TPU v7x, 32 devices: a whole 2x2x4 slice. The times are simulated.
32 devices in a mesh: section: 2 (over core), dp: 16 (over z, y, x).
Axes of the slice: x: 2, y: 2, z: 4, core: 2. Of those that a mesh axis runs over, the one named last changes fastest.
Arguments:
- frames: bfloat16 [16, 1024, 80], P('dp'), may hold values from -6 to 6
- targets: int32 [16, 1024], P('dp'), may hold values from 0 to 1023
- lengths: int32 [16], P('dp'), may hold values from 128 to 1024, as said below
- w_attn: float32 [2, 512, 1536], P('section', 'dp'), may hold values from -0.25 to 0.25
- w_out: float32 [2, 512, 512], P('section', 'dp'), may hold values from -0.75 to 0.75
- w_pos: float32 [2, 512, 512], P('section', 'dp'), may hold values from -0.25 to 0.25
- w_up: float32 [2, 512, 2048], P('section', 'dp'), may hold values from -0.25 to 0.25
- w_down: float32 [2, 2048, 512], P('section', 'dp'), may hold values from -0.125 to 0.125
- layer_vecs: float32 [2, 4, 512], P('section', None, 'dp'), may hold values from -1.5 to 3.125
- w_in: float32 [80, 512], P(None, 'dp'), may hold values from -0.625 to 0.625
- w_head: float32 [512, 1024], P('dp'), may hold values from -0.25 to 0.25
- gain_final: float32 [512], P('dp'), may hold values from 0.4 to 3.125
- moment_attn: float32 [2, 512, 1536], P('section', 'dp'), may hold values from -4.7683716e-06 to 4.7683716e-06
- moment_out: float32 [2, 512, 512], P('section', 'dp'), may hold values from -4.7683716e-06 to 4.7683716e-06
- moment_pos: float32 [2, 512, 512], P('section', 'dp'), may hold values from -4.7683716e-06 to 4.7683716e-06
- moment_up: float32 [2, 512, 2048], P('section', 'dp'), may hold values from -4.7683716e-06 to 4.7683716e-06
- moment_down: float32 [2, 2048, 512], P('section', 'dp'), may hold values from -4.7683716e-06 to 4.7683716e-06
- moment_vecs: float32 [2, 4, 512], P('section', None, 'dp'), may hold values from -1.9073486e-05 to 1.9073486e-05
- moment_in: float32 [80, 512], P(None, 'dp'), may hold values from -4.7683716e-06 to 4.7683716e-06
- moment_head: float32 [512, 1024], P('dp'), may hold values from -4.7683716e-06 to 4.7683716e-06
- moment_final: float32 [512], P('dp'), may hold values from -1.9073486e-05 to 1.9073486e-05
- second_attn: float32 [2, 512, 1536], P('section', 'dp'), may hold values from 5.4159446e-14 to 2.1663778e-13
- second_out: float32 [2, 512, 512], P('section', 'dp'), may hold values from 5.4159446e-14 to 2.1663778e-13
- second_pos: float32 [2, 512, 512], P('section', 'dp'), may hold values from 2.7079722e-15 to 1.0831889e-14
- second_up: float32 [2, 512, 2048], P('section', 'dp'), may hold values from 5.4159446e-14 to 2.1663778e-13
- second_down: float32 [2, 2048, 512], P('section', 'dp'), may hold values from 5.4159446e-14 to 2.1663778e-13
- second_vecs: float32 [2, 4, 512], P('section', None, 'dp'), may hold values from 8.6655113e-13 to 3.4662045e-12
- second_in: float32 [80, 512], P(None, 'dp'), may hold values from 5.4159446e-14 to 2.1663778e-13
- second_head: float32 [512, 1024], P('dp'), may hold values from 5.4159446e-14 to 2.1663778e-13
- second_final: float32 [512], P('dp'), may hold values from 8.6655113e-13 to 3.4662045e-12
Outputs:
- new_attn: float32 [2, 512, 1536], P('section', 'dp')
- new_out: float32 [2, 512, 512], P('section', 'dp')
- new_pos: float32 [2, 512, 512], P('section', 'dp')
- new_up: float32 [2, 512, 2048], P('section', 'dp')
- new_down: float32 [2, 2048, 512], P('section', 'dp')
- new_vecs: float32 [2, 4, 512], P('section', None, 'dp')
- new_in: float32 [80, 512], P(None, 'dp')
- new_head: float32 [512, 1024], P('dp')
- new_final: float32 [512], P('dp')
- new_moment_attn: float32 [2, 512, 1536], P('section', 'dp')
- new_moment_out: float32 [2, 512, 512], P('section', 'dp')
- new_moment_pos: float32 [2, 512, 512], P('section', 'dp')
- new_moment_up: float32 [2, 512, 2048], P('section', 'dp')
- new_moment_down: float32 [2, 2048, 512], P('section', 'dp')
- new_moment_vecs: float32 [2, 4, 512], P('section', None, 'dp')
- new_moment_in: float32 [80, 512], P(None, 'dp')
- new_moment_head: float32 [512, 1024], P('dp')
- new_moment_final: float32 [512], P('dp')
- new_second_attn: float32 [2, 512, 1536], P('section', 'dp')
- new_second_out: float32 [2, 512, 512], P('section', 'dp')
- new_second_pos: float32 [2, 512, 512], P('section', 'dp')
- new_second_up: float32 [2, 512, 2048], P('section', 'dp')
- new_second_down: float32 [2, 2048, 512], P('section', 'dp')
- new_second_vecs: float32 [2, 4, 512], P('section', None, 'dp')
- new_second_in: float32 [80, 512], P(None, 'dp')
- new_second_head: float32 [512, 1024], P('dp')
- new_second_final: float32 [512], P('dp')
- grad_norm: float32 [], replicated
- loss_sum: float32 [], replicated
Inputs may be any that keep to these rules, and one draw needn't show every extreme that they name: `lengths`: one stream has exactly 1024 valid frames.
All inputs are finite; a program needn't handle non-finite values.
Results may differ from a plain program's by a relative error of at most 0.012.
The roundings to bfloat16 on the way count: a program that leaves them out, or rounds other values in their place, can miss the bound.
Values may be sent and summed in bfloat16 or wider, within the bound.
No kernel may reach another device: no remote copies, remote signals or barrier semaphores. Data moves between devices by JAX's collectives and lax.ppermute only.
A program may use at most 192 MiB of HBM per device.

v0:
```python
import functools

import jax
import jax.numpy as jnp
from jax import lax
from jax.experimental import pallas as pl
from jax.experimental.pallas import tpu as pltpu
from jax.sharding import PartitionSpec as P

D = 512
FF = 2048
CODES = 1024
FEATS = 80
MEM = 256
SEG = 512
SEGS = 2
STEP = 10
ROWS = MEM + SEG
BLOCK = 128
PAIRS = 4
WIDE = 18 * BLOCK
GROUPS = 16
QUERY_U_AT, QUERY_V_AT, KEYS_AT, VALUES_AT, REL_AT, WEIGHTS_AT, SMALL_AT = 768, 1280, 1792, 2560, 3328, 4096, 6144
ACTIVE_AT, SLOPE_AT, UP_AT, DOWN_AT, OUT_AT = 512, 2560, 4608, 6656, 8704
KEPT_ROWS = 16384
KEPT_PAIRS = 14
IN_ORDER = ((1, 2, 4, 8), (1, 2, 4, 8))
NEG = -1e30
CLIP = 0.02
SCALE = 0.125
F32 = jnp.float32
BF16 = jnp.bfloat16
SPANS = tuple((MEM + BLOCK * (b + 1) for b in range(4)))
STARTS = tuple((sum(SPANS[:b]) for b in range(4)))


def nn(left, right):
    return jnp.dot(left, right, preferred_element_type=F32)


def nt(left, right):
    return lax.dot_general(left, right, (((1,), (1,)), ((), ())), preferred_element_type=F32)


def tn(left, right):
    return lax.dot_general(left, right, (((0,), (0,)), ((), ())), preferred_element_type=F32)


def norm_parts(values):
    center = values - jnp.mean(values, -1, keepdims=True)
    spread = jnp.mean(center * center, -1, keepdims=True)
    inverse = lax.rsqrt(spread + 1e-05)
    return center * inverse, inverse


def norm_back(unit, inverse, gain, grad):
    scaled = grad * gain
    first = jnp.mean(scaled, -1, keepdims=True)
    second = jnp.mean(scaled * unit, -1, keepdims=True)
    return inverse * (scaled - first - unit * second), jnp.sum(grad * unit, 0, keepdims=True)


def group_of(bits, spot, place, half):
    if bits == IN_ORDER:
        return spot
    low, high = (sum((bit for index, bit in enumerate(each) if (spot >> index) & 1)) for each in bits)
    return jnp.bitwise_xor(place, low if low == high else jnp.where(half == 0, low, high))


def copies(bits, place, half, pieces, units, rows, sem, outward):
    count = GROUPS // len(pieces)
    for index, slab in enumerate(pieces):
        for spot in range(count):
            group = group_of(bits, index * count + spot, place, half)
            for whole, first in units:
                there = whole.at[pl.ds(pl.multiple_of((group * 2 + half) * rows, rows), rows), :]
                here = slab.at[spot, pl.ds(first, rows), pl.ds(0, whole.shape[1])]
                if outward:
                    pltpu.make_async_copy(there, here, sem).start()
                else:
                    pltpu.make_async_copy(here, there, sem).start()


def columns(ref, count):
    return [ref.at[:, pl.ds(D * u, D)] for u in range(count)]


def fetch(source, target, sem):
    copy = pltpu.make_async_copy(source, target, sem)
    copy.start()
    return copy


def arrived(buffer, sem):
    pltpu.make_async_copy(buffer, buffer, sem).wait()


def tri_mask():
    row = lax.broadcasted_iota(jnp.int32, (2 * BLOCK, BLOCK), 0)
    col = lax.broadcasted_iota(jnp.int32, (2 * BLOCK, BLOCK), 1)
    return col <= lax.rem(row, BLOCK)


def stack_heads(part):
    col = lax.broadcasted_iota(jnp.int32, part.shape, 1)
    zero = jnp.zeros_like(part)
    return jnp.concatenate(
        [jnp.where(col < 64, part, zero), jnp.where(col < 64, zero, part)], 0
    )


def pick_heads(both):
    col = lax.broadcasted_iota(jnp.int32, (BLOCK, BLOCK), 1)
    return jnp.where(col < 64, both[:BLOCK], both[BLOCK:])


def shift(both, amount):
    return jnp.concatenate(
        [pltpu.roll(part, amount, 1, stride=1, stride_axis=0) for part in (both[:BLOCK], both[BLOCK:])], 0
    )


def masked(score, triangle, first):
    if first == 0:
        return jnp.where(triangle, score, NEG)
    return jnp.concatenate([score[:, :first], jnp.where(triangle, score[:, first:], NEG)], 1)


def lanes(pair):
    return pl.ds(pl.multiple_of(pair * BLOCK, BLOCK), BLOCK)


def project(bits, base, *refs):
    first_layer = base == 0
    if first_layer:
        (scalars, frames, own_low, own_high, other_low, other_high, table) = refs[:7]
        (query_u, query_v, keys, values, rel, hidden, vecs, saved) = refs[7:15]
        (normed, weights, in_sem, out_sem, joined, small, small_sem) = refs[15:]
    else:
        (scalars, memory, hidden, vecs, own_low, own_high, other_low, other_high, table) = refs[:9]
        (query_u, query_v, keys, values, rel, saved) = refs[9:15]
        (normed, weights, in_sem, out_sem) = refs[15:]
    place, half = scalars[0], scalars[1]
    both = ((half, (own_low, own_high)), (1 - half, (other_low, other_high)))
    if first_layer:
        for which, pieces in both:
            copies(bits, place, which, pieces, [(small, 64)], 16, small_sem, False)
    units = [(weights.at[u], 16 * u) for u in range(4)]
    for which, pieces in both:
        copies(bits, place, which, pieces, units, 16, in_sem, False)
    if first_layer:
        arrived(small, small_sem)
        small_out = fetch(small, saved.at[pl.ds(SMALL_AT, D), pl.ds(0, BLOCK)], out_sem.at[7])
        vecs[...] = jnp.transpose(small[...].astype(F32))[80:96]
        for b in range(3):
            rows = pl.ds(256 * b, 256)
            joined[rows, :] = nt(frames[rows, :], small[...])
        hidden[...] = joined[MEM:, :]
        sources = [joined.at[pl.ds(256 * b, 256)] for b in range(3)]
    else:
        sources = [memory, hidden.at[pl.ds(0, 256)], hidden.at[pl.ds(256, 256)]]
    gain = vecs[base : base + 1, :]
    bias_u = vecs[base + 2 : base + 3, :]
    bias_v = vecs[base + 3 : base + 4, :]
    arrived(weights, in_sem)
    outs = [fetch(weights.at[u], saved.at[pl.ds(WEIGHTS_AT + D * u, D)], out_sem.at[8 + u]) for u in range(4)]
    rel[...] = nn(table[...], weights[3]).astype(BF16)
    outs.append(fetch(rel, saved.at[pl.ds(REL_AT, ROWS)], out_sem.at[5]))
    for b in range(3):
        unit, unused = norm_parts(sources[b][...])
        normed[pl.ds(256 * b, 256), :] = (unit * gain).astype(BF16)
    outs.append(fetch(normed, saved.at[pl.ds(0, ROWS)], out_sem.at[0]))
    keys[...] = nn(normed[...], weights[1]).astype(BF16)
    outs.append(fetch(keys, saved.at[pl.ds(KEYS_AT, ROWS)], out_sem.at[3]))
    values[...] = nn(normed[...], weights[2]).astype(BF16)
    outs.append(fetch(values, saved.at[pl.ds(VALUES_AT, ROWS)], out_sem.at[4]))
    query = nn(normed[MEM:, :], weights[0])
    query_u[...] = (query + bias_u).astype(BF16)
    query_v[...] = (query + bias_v).astype(BF16)
    outs.append(fetch(query_u, saved.at[pl.ds(QUERY_U_AT, SEG)], out_sem.at[1]))
    outs.append(fetch(query_v, saved.at[pl.ds(QUERY_V_AT, SEG)], out_sem.at[2]))
    if first_layer:
        outs.append(small_out)
    for copy in outs:
        copy.wait()


def attend(scalars, query_u, query_v, keys, values, rel, attended, probs_o, probs, out_sem):
    length, segment = scalars[2], scalars[3]
    spot = lax.broadcasted_iota(jnp.int32, (1, ROWS), 1)
    where_at = segment * SEG + spot - MEM
    allowed = (where_at < length) & ((spot >= MEM) | (segment >= 1))
    bias = jnp.where(allowed, 0.0, NEG)
    triangle = tri_mask()

    def two_pairs(first, step, carry):
        tiles = [(2 * step + one, b, SPANS[b] - first) for one in range(2) for b in range(4)]
        full = [
            nt(stack_heads(query_v[BLOCK * b : BLOCK * (b + 1), lanes(pair)]) * SCALE,
               rel[ROWS - span : ROWS, lanes(pair)])
            for pair, b, span in tiles
        ]
        content = [
            nt(stack_heads(query_u[BLOCK * b : BLOCK * (b + 1), lanes(pair)]) * SCALE,
               keys[first : first + span, lanes(pair)])
            for pair, b, span in tiles
        ]
        full = [shift(item, span - BLOCK + 1) for item, (pair, b, span) in zip(full, tiles)]
        score = [
            masked(one + two + bias[:, first : first + span], triangle, span - BLOCK)
            for one, two, (pair, b, span) in zip(content, full, tiles)
        ]
        top = [jnp.max(item, -1, keepdims=True) for item in score]
        expo = [jnp.exp(item - most) for item, most in zip(score, top)]
        total = [jnp.sum(item, -1, keepdims=True) for item in expo]
        prob = [(item * (1.0 / most)).astype(BF16) for item, most in zip(expo, total)]
        for item, (pair, b, span) in zip(prob, tiles):
            probs[pair, :, STARTS[b] + first : STARTS[b] + first + span] = item
        for one in range(2):
            pair = 2 * step + one
            pltpu.make_async_copy(probs.at[pair], probs_o.at[pair], out_sem.at[pair]).start()
        found = [
            nn(item, values[first : first + span, lanes(pair)]) for item, (pair, b, span) in zip(prob, tiles)
        ]
        for item, (pair, b, span) in zip(found, tiles):
            attended[BLOCK * b : BLOCK * (b + 1), lanes(pair)] = pick_heads(item).astype(BF16)
        return carry

    for first in (0, MEM):

        @pl.when((segment == 0) == (first > 0))
        def _():
            lax.fori_loop(0, PAIRS // 2, functools.partial(two_pairs, first), 0)

    outs = [
        fetch(attended.at[pl.ds(256 * b, 256)], probs_o.at[PAIRS + b, :, pl.ds(0, D)], out_sem.at[PAIRS + b])
        for b in range(2)
    ]
    for pair in range(PAIRS):
        pltpu.make_async_copy(probs.at[pair], probs_o.at[pair], out_sem.at[pair]).wait()
    for copy in outs:
        copy.wait()


def attend_back(bits, second, *refs):
    (scalars, grad_att, table_h, saved, probs_h) = refs[:5]
    normed, table, late_sem = refs[-3:]
    rest = refs[5:-3]
    query_u_h, query_v_h, keys_h, values_h, rel_h = (
        saved.at[pl.ds(first, rows)]
        for first, rows in (
            (QUERY_U_AT, SEG), (QUERY_V_AT, SEG), (KEYS_AT, ROWS), (VALUES_AT, ROWS), (REL_AT, ROWS)
        )
    )
    if second:
        staged_h = rest[0]
        rest = rest[1:]
        (keep, send) = rest[4:6]
        sums, rest = rest[3], rest[:3] + rest[6:]
    else:
        (staged, sums) = rest[3:5]
        rest = rest[:3] + rest[5:]
    (grad_query, grad_keys, grad_values,
     query_u, query_v, keys, values, rel, probs, flip, acc_keys, acc_values, acc_rel,
     grad_qu, grad_qv, pair_sem) = rest[:16]
    first_pair = 2 if second else 0

    def parts(pair):
        lane, here = lanes(pair + first_pair), lanes(pair)
        moves = [(probs_h.at[pair + first_pair], probs.at[pair])]
        for there, target in (
            (query_u_h, query_u), (query_v_h, query_v), (keys_h, keys), (values_h, values), (rel_h, rel)
        ):
            moves.append((there.at[:, lane], target.at[:, here]))
        return [
            pltpu.make_async_copy(there, target, pair_sem.at[pair, index])
            for index, (there, target) in enumerate(moves)
        ]

    for pair in range(2):
        for copy in parts(pair):
            copy.start()
    late = [fetch(saved.at[pl.ds(0, ROWS)], normed, late_sem.at[0]), fetch(table_h, table, late_sem.at[1])]
    if second:
        staged, sem = rest[16:]
        staged[:, :, 0:256] = staged_h[...]
    row = lax.broadcasted_iota(jnp.int32, (2 * BLOCK, 2 * BLOCK), 0)
    col = lax.broadcasted_iota(jnp.int32, (2 * BLOCK, 2 * BLOCK), 1)
    back = (row // BLOCK) * BLOCK + BLOCK - 1 - lax.rem(row, BLOCK)
    flip[...] = (col == back).astype(F32).astype(BF16)

    segment = scalars[3]

    def one_pair(first, pair, carry):
        lane = lanes(pair)
        for copy in parts(pair):
            copy.wait()
        order = (3, 2, 1, 0)
        flipped = flip[...]
        stack_g = [
            stack_heads(grad_att[BLOCK * b : BLOCK * (b + 1), lanes(pair + first_pair)]) for b in order
        ]
        stack_u = [stack_heads(query_u[BLOCK * b : BLOCK * (b + 1), lane]) * SCALE for b in order]
        stack_v = [
            nn(flipped, stack_heads(query_v[BLOCK * b : BLOCK * (b + 1), lane]) * SCALE).astype(BF16)
            for b in order
        ]
        spans = [SPANS[b] - first for b in order]
        prob_b = [
            probs[pair, :, STARTS[b] + first : STARTS[b] + first + span] for b, span in zip(order, spans)
        ]
        grad_prob = [nt(one, values[first : first + span, lane]) for one, span in zip(stack_g, spans)]
        part_values = [tn(one, two) for one, two in zip(stack_g, prob_b)]
        prob = [item.astype(F32) for item in prob_b]
        inner = [jnp.sum(one * two, -1, keepdims=True) for one, two in zip(prob, grad_prob)]
        grad_score = [
            (one * (two - three)).astype(BF16) for one, two, three in zip(prob, grad_prob, inner)
        ]
        turned = [nn(flipped, item) for item in grad_score]
        found_u = [nn(item, keys[first : first + span, lane]) for item, span in zip(grad_score, spans)]
        part_keys = [tn(one, two) for one, two in zip(stack_u, grad_score)]
        grad_full = [shift(item, 0).astype(BF16) for item in turned]
        found_v = [nn(item, rel[ROWS - span : ROWS, lane]) for item, span in zip(grad_full, spans)]
        part_rel = [tn(one, two) for one, two in zip(stack_v, grad_full)]
        for index, b in enumerate(order):
            span = spans[index]
            rows = pl.ds(BLOCK * b, BLOCK)
            grad_qu[rows, lane] = pick_heads(found_u[index]) * SCALE
            grad_qv[rows, lane] = pick_heads(found_v[index]) * SCALE
            if b == 3:
                acc_keys[lane, first:] = part_keys[index]
                acc_values[lane, first:] = part_values[index]
                acc_rel[lane, ROWS - span :] = part_rel[index]
                if first:
                    blank = jnp.zeros((BLOCK, first), F32)
                    acc_keys[lane, 0:first] = blank
                    acc_values[lane, 0:first] = blank
                    acc_rel[lane, 0 : ROWS - span] = blank
            else:
                acc_keys[lane, first : first + span] += part_keys[index]
                acc_values[lane, first : first + span] += part_values[index]
                acc_rel[lane, ROWS - span : ROWS] += part_rel[index]
        return carry

    for first in (0, MEM):

        @pl.when((segment == 0) == (first > 0))
        def _():
            lax.fori_loop(0, 2, functools.partial(one_pair, first), 0)

    grad_keys[...] = jnp.transpose(acc_keys[...]).astype(BF16)
    grad_values[...] = jnp.transpose(acc_values[...]).astype(BF16)
    grad_rel = jnp.transpose(acc_rel[...]).astype(BF16)
    sums[...] = jnp.zeros_like(sums)
    sums[2:3, :] = jnp.sum(grad_qu[...], 0, keepdims=True)
    sums[3:4, :] = jnp.sum(grad_qv[...], 0, keepdims=True)
    flip_one = flip[0:BLOCK, 0:BLOCK]
    for b in range(4):
        rows = pl.ds(BLOCK * b, BLOCK)
        part = grad_qv[rows, :]
        high = part.astype(BF16)
        low = (part - high.astype(F32)).astype(BF16)
        grad_query[rows, :] = (grad_qu[rows, :] + nn(flip_one, high) + nn(flip_one, low)).astype(BF16)
    for copy in late:
        copy.wait()
    cols = slice(256, 512) if second else slice(None)
    staged[1, :, cols] = tn(normed[...], grad_keys[...]).astype(BF16)
    staged[2, :, cols] = tn(normed[...], grad_values[...]).astype(BF16)
    staged[3, :, cols] = tn(table[...], grad_rel).astype(BF16)
    staged[0, :, cols] = tn(normed[MEM:, :], grad_query[...]).astype(BF16)
    if second:
        place, half = scalars[0], scalars[1]
        units = [(staged.at[u], 16 * u) for u in range(4)]
        copies(bits, place, half, (keep,), units, 16, sem, True)
        copies(bits, place, 1 - half, (send,), units, 16, sem, True)
        arrived(staged, sem)


def input_grads(bits, base, *refs):
    last_kernel = base == 0
    weights, weights_sem = refs[-2:]
    refs = refs[:-2]
    weights_copies = [
        fetch(refs[1].at[pl.ds(WEIGHTS_AT + D * u, D)], weights.at[u], weights_sem.at[u]) for u in range(3)
    ]
    (scalars, saved, query_a, keys_a, values_a, sums_a, query_b, keys_b, values_b, sums_b, grad_mixed, vecs) = refs[:12]
    if last_kernel:
        (frames, gain_two, vecs_one, gain_two_one, gain_final, keep, send,
         joined, smalls, staged, sem, small, small_sem) = refs[12:]
        fetch(saved.at[pl.ds(SMALL_AT, D), pl.ds(0, BLOCK)], small, small_sem).wait()
        joined[...] = nt(frames[...], small[...])
        before, here, first = joined, joined, MEM
    else:
        (memory, hidden, grad_hidden, grad_vecs) = refs[12:]
        before, here, first = memory, hidden, 0
    place, half = scalars[0], scalars[1]
    gain = vecs[base : base + 1, :]
    left, right = slice(0, 256), slice(256, 512)
    for copy in weights_copies:
        copy.wait()
    grad_keys = (
        nt(keys_a[...], weights[1, :, left])
        + nt(keys_b[...], weights[1, :, right])
        + nt(values_a[...], weights[2, :, left])
        + nt(values_b[...], weights[2, :, right])
    )
    grad_query = nt(query_a[...], weights[0, :, left]) + nt(query_b[...], weights[0, :, right])
    unit, inverse = norm_parts(before[0:MEM, :])
    grad_gain = jnp.sum(grad_keys[0:MEM] * unit, 0, keepdims=True)
    unit, inverse = norm_parts(here[first : first + SEG, :])
    grad_joined, gains = norm_back(unit, inverse, gain, grad_keys[MEM:] + grad_query)
    grad_gain = grad_gain + gains
    grad_in = grad_mixed[...] + grad_joined
    if last_kernel:
        smalls[...] = tn(frames[MEM:, :], grad_in.astype(BF16))
        smalls[80:81, :] = grad_gain
        smalls[81:82, :] = gain_two[0:1, :]
        smalls[82:84, left] = sums_a[2:4, :]
        smalls[82:84, right] = sums_b[2:4, :]
        smalls[84:88, :] = vecs_one[0:4, :]
        smalls[85:86, :] = gain_two_one[0:1, :]
        smalls[88:89, :] = gain_final[0:1, :]
        staged[...] = jnp.zeros_like(staged)
        staged[:, 0:BLOCK] = jnp.transpose(smalls[...]).astype(BF16)
        units = [(staged, 0)]
        copies(bits, place, half, (keep,), units, 16, sem, True)
        copies(bits, place, 1 - half, (send,), units, 16, sem, True)
        arrived(staged, sem)
    else:
        grad_hidden[...] = grad_in
        grad_vecs[:, left] = sums_a[...]
        grad_vecs[:, right] = sums_b[...]
        grad_vecs[0:1, :] = grad_gain


def feed_weights(bits, place, both, up, down, out, sem):
    for index, (units, rows) in enumerate(
        (
            ([(out, 128)], 16),
            ([(item, 16 * u) for u, item in enumerate(columns(up, 4))], 16),
            ([(down, 64)], 64),
        )
    ):
        for which, pieces in both:
            copies(bits, place, which, pieces, units, rows, sem.at[index], False)


def feed_mixed(residual, attended, out, gain, mixed, normed):
    mixed[...] = residual[...] + nn(attended[...], out[...])
    for b in range(2):
        rows = pl.ds(256 * b, 256)
        unit, unused = norm_parts(mixed[rows, :])
        normed[rows, :] = (unit * gain).astype(BF16)


def feed_inner(normed, up, active, slope):
    later = nn(normed[...], up[:, 0:512])
    for u in range(4):
        inner = later
        if u < 3:
            later = nn(normed[...], up[:, 512 * (u + 1) : 512 * (u + 2)])
        square = inner * inner
        bent = jnp.tanh(0.7978845608028654 * (inner + 0.044715 * (square * inner)))
        half = 0.5 * (1.0 + bent)
        active[:, 512 * u : 512 * (u + 1)] = (inner * half).astype(BF16)
        slope[:, 512 * u : 512 * (u + 1)] = (
            half
            + (0.5 * inner)
            * (1.0 - bent * bent)
            * (0.7978845608028654 * (1.0 + (3 * 0.044715) * square))
        ).astype(BF16)


def feed_output(mixed, active, down, output):
    output[...] = mixed[...] + nn(active[...], down[...])


def feed_forward(bits, base, scalars, residual, attended, vecs, own_low, own_high, other_low, other_high,
                 output, memory, mixed_o, saved,
                 mixed, normed, active, slope, up, down, out, sem, out_sem):
    place, half = scalars[0], scalars[1]
    both = ((half, (own_low, own_high)), (1 - half, (other_low, other_high)))
    feed_weights(bits, place, both, up, down, out, sem)
    arrived(out, sem.at[0])
    outs = [fetch(out, saved.at[pl.ds(OUT_AT, D)], out_sem.at[0])]
    feed_mixed(residual, attended, out, vecs[base + 1 : base + 2, :], mixed, normed)
    outs.append(fetch(normed, saved.at[pl.ds(0, SEG)], out_sem.at[1]))
    outs.append(fetch(mixed, mixed_o, out_sem.at[2]))
    arrived(up, sem.at[1])
    outs += [
        fetch(item, saved.at[pl.ds(UP_AT + D * u, D)], out_sem.at[4 + u])
        for u, item in enumerate(columns(up, 4))
    ]
    feed_inner(normed, up, active, slope)
    for u in range(4):
        cols = pl.ds(D * u, D)
        outs.append(fetch(active.at[:, cols], saved.at[pl.ds(ACTIVE_AT + D * u, D)], out_sem.at[8 + u]))
        outs.append(fetch(slope.at[:, cols], saved.at[pl.ds(SLOPE_AT + D * u, D)], out_sem.at[12 + u]))
    arrived(down, sem.at[2])
    outs.append(fetch(down, saved.at[pl.ds(DOWN_AT, FF)], out_sem.at[3]))
    feed_output(mixed, active, down, output)
    memory[...] = output[SEG - MEM :, :]
    for copy in outs:
        copy.wait()


def feed_back(moves, bits, place, half, keep, send, sem, base, grad_out, mixed, vecs, attended, normed,
              active, slope, up, down, out, grad_mixed, grad_att, grad_gain,
              grad_inner, staged_up, staged_down, staged_out):
    both = ((half, (keep,)), (1 - half, (send,)))
    grad_y = grad_out[...].astype(BF16)
    for copy in moves[:1]:
        copy.wait()
    later = nt(grad_y, down[0:512, :])
    for copy in moves[1:10]:
        copy.wait()
    for u in range(4):
        cols = slice(512 * u, 512 * (u + 1))
        part = later
        if u < 3:
            later = nt(grad_y, down[512 * (u + 1) : 512 * (u + 2), :])
        staged_down[cols, :] = tn(active[:, cols], grad_y).astype(BF16)
        grad_inner[:, cols] = (part * slope[:, cols].astype(F32)).astype(BF16)
    for copy in moves[10:]:
        copy.wait()
    grad_normed = nt(grad_inner[...], up[...])
    for which, pieces in both:
        copies(bits, place, which, pieces, [(staged_down, 64)], 64, sem.at[1], True)
    for u in range(4):
        cols = slice(512 * u, 512 * (u + 1))
        staged_up[:, cols] = tn(normed[...], grad_inner[:, cols]).astype(BF16)
    unit, inverse = norm_parts(mixed[...])
    grad_here, gains = norm_back(unit, inverse, vecs[base + 1 : base + 2, :], grad_normed)
    grad = grad_out[...] + grad_here
    grad_mixed[...] = grad
    grad_b = grad.astype(BF16)
    for which, pieces in both:
        units = [(item, 16 * u) for u, item in enumerate(columns(staged_up, 4))]
        copies(bits, place, which, pieces, units, 16, sem.at[0], True)
    grad_att[...] = nt(grad_b, out[...]).astype(BF16)
    staged_out[...] = tn(attended[...], grad_b).astype(BF16)
    for which, pieces in both:
        copies(bits, place, which, pieces, [(staged_out, 128)], 16, sem.at[2], True)
    grad_gain[...] = jnp.broadcast_to(gains, grad_gain.shape)
    arrived(staged_up, sem.at[0])
    arrived(staged_down, sem.at[1])
    arrived(staged_out, sem.at[2])


def feed_backward(bits, base, scalars, grad_out, vecs, mixed_h, probs_h, saved,
                  keep, send, grad_mixed, grad_att, grad_gain, mixed, attended,
                  normed, active, slope, up, down, out, grad_inner, staged_up, staged_down, staged_out,
                  in_sem, sem):
    pairs = [(saved.at[pl.ds(DOWN_AT, FF)], down)]
    for u in range(4):
        pairs.append((saved.at[pl.ds(SLOPE_AT + D * u, D)], slope.at[:, pl.ds(D * u, D)]))
    for u in range(4):
        pairs.append((saved.at[pl.ds(ACTIVE_AT + D * u, D)], active.at[:, pl.ds(D * u, D)]))
    pairs.append((saved.at[pl.ds(0, SEG)], normed))
    for u in range(4):
        pairs.append((saved.at[pl.ds(UP_AT + D * u, D)], columns(up, 4)[u]))
    pairs.append((saved.at[pl.ds(OUT_AT, D)], out))
    pairs.append((mixed_h, mixed))
    for b in range(2):
        pairs.append((probs_h.at[PAIRS + b, :, pl.ds(0, D)], attended.at[pl.ds(256 * b, 256)]))
    moves = [fetch(there, here, in_sem.at[index]) for index, (there, here) in enumerate(pairs)]
    feed_back(moves, bits, scalars[0], scalars[1], keep, send, sem, base, grad_out, mixed, vecs, attended, normed,
              active, slope, up, down, out, grad_mixed, grad_att, grad_gain,
              grad_inner, staged_up, staged_down, staged_out)


def top_kernel(bits, streams, scalars, residual, attended, targets, vecs, own_low, own_high, other_low, other_high,
               keep, send, grad_mixed, grad_att, grad_gain, final_gain, loss,
               normed, active, slope, up, down, out, mixed, output, grad_out, table, final, grad_logits, staged,
               grad_inner, staged_up, staged_down, staged_out, head_sem, sem, out_sem):
    place, half, length, segment = scalars[0], scalars[1], scalars[2], scalars[3]
    both = ((half, (own_low, own_high)), (1 - half, (other_low, other_high)))
    feed_weights(bits, place, both, up, down, out, sem)
    units = [(item, 144 + 16 * u) for u, item in enumerate(columns(table, 2))]
    for which, pieces in both:
        copies(bits, place, which, pieces, units, 16, head_sem, False)
    arrived(out, sem.at[0])
    feed_mixed(residual, attended, out, vecs[5:6, :], mixed, normed)
    arrived(up, sem.at[1])
    feed_inner(normed, up, active, slope)
    arrived(down, sem.at[2])
    feed_output(mixed, active, down, output)
    arrived(table, head_sem)
    size = length.astype(F32)
    codes = jnp.transpose(jnp.broadcast_to(targets[...].astype(F32), (BLOCK, SEG))).astype(jnp.int32)
    gain = vecs[8:9, :]
    gains = jnp.zeros((1, D), F32)
    terms = jnp.zeros((1, 1), F32)
    spans = (slice(0, 256), slice(256, 512))
    parts = [norm_parts(output[rows, :]) for rows in spans]
    fins = [(unit * gain).astype(BF16) for unit, unused in parts]
    logits = [nn(fin, table[...]) for fin in fins]
    for rows, fin in zip(spans, fins):
        final[rows, :] = fin
    grad_finals = []
    for b, rows in enumerate(spans):
        logit = logits[b]
        most = jnp.max(logit, -1, keepdims=True)
        expo = jnp.exp(logit - most)
        total = jnp.sum(expo, -1, keepdims=True)
        picks = lax.broadcasted_iota(jnp.int32, logit.shape, 1) == codes[rows, 0:1]
        picked = jnp.sum(jnp.where(picks, logit, 0.0), -1, keepdims=True)
        spot = segment * SEG + 256 * b + lax.broadcasted_iota(jnp.int32, (256, 1), 0)
        weight = jnp.where(spot < length, 1.0 / size, 0.0)
        terms = terms + jnp.sum((most + jnp.log(total) - picked) * weight, keepdims=True)
        grad = (expo * (1.0 / total) - jnp.where(picks, 1.0, 0.0)) * (weight * (1.0 / streams))
        grad_logits[rows, :] = grad.astype(BF16)
        grad_finals.append(nt(grad_logits[rows, :], table[...]))
    staged[...] = tn(final[...], grad_logits[...]).astype(BF16)
    for (unit, inverse), rows, grad_final in zip(parts, spans, grad_finals):
        grad_here, gain_here = norm_back(unit, inverse, gain, grad_final)
        grad_out[rows, :] = grad_here
        gains = gains + gain_here
    units = [(item, 144 + 16 * u) for u, item in enumerate(columns(staged, 2))]
    copies(bits, place, half, (keep,), units, 16, head_sem, True)
    copies(bits, place, 1 - half, (send,), units, 16, head_sem, True)
    final_gain[...] = jnp.broadcast_to(gains, final_gain.shape)
    loss[...] = jnp.broadcast_to(terms, loss.shape)
    feed_back((), bits, place, half, keep, send, out_sem, 4, grad_out, mixed, vecs, attended, normed,
              active, slope, up, down, out, grad_mixed, grad_att, grad_gain,
              grad_inner, staged_up, staged_down, staged_out)
    arrived(staged, head_sem)


def finish(counts, *refs):
    scalars, loss = refs[0], refs[1]
    total_count = sum(counts)
    sources = refs[2 : 2 + total_count]
    kept, sent, total = refs[2 + total_count : 5 + total_count]
    buffers, sem = refs[5 + total_count : -1], refs[-1]
    moves = [fetch(there.at[0], here, sem.at[index]) for index, (there, here) in enumerate(zip(sources, buffers))]
    for copy in moves:
        copy.wait()
    sums = []
    start = 0
    for count in counts:
        item = buffers[start][...].astype(F32)
        for other in buffers[start + 1 : start + count]:
            item = item + other[...].astype(F32)
        sums.append(item)
        start += count
    attn_zero, feed_zero, attn_one, feed_one, small = sums[0], sums[1], sums[2], sums[3], sums[4]
    attn_zero = attn_zero + sums[5][0:64]
    small = small + sums[5][64:80]
    first = scalars[1] == 0
    lone = jnp.zeros((1, 1), F32)
    for zero, one, rows, begin in ((attn_zero, attn_one, 64, 0), (feed_zero, feed_one[0:144], 144, 64)):
        kept[begin : begin + rows, :] = jnp.where(first, zero, one)
        sent[begin : begin + rows, :] = jnp.where(first, one, zero)
        lone = lone + jnp.sum(zero * zero + one * one, keepdims=True)
    head = feed_one[144:176]
    lone = lone + jnp.sum(head * head, keepdims=True) + jnp.sum(small * small, keepdims=True)
    for target in (kept, sent):
        target[208:240, :] = head
        target[240:256, :] = small
    column = lax.broadcasted_iota(jnp.int32, (8, 128), 1)
    total[...] = jnp.where(column == 0, lone, 0.0) + jnp.where(column == 1, loss[...], 0.0)


def adam_step(weight, grad, first, second, rate, decay, factor):
    grad = grad * factor
    first = 0.9 * first + 0.1 * grad
    second = 0.999 * second + 0.001 * grad * grad
    ratio = first / (1.0 - 0.9**STEP) / (jnp.sqrt(second / (1.0 - 0.999**STEP)) + 1e-08)
    return (weight - rate * (ratio + decay * weight), first, second)


def update(scalars, total, kept, got, *refs):
    ins, outs, small = refs[:27], refs[27:56], refs[56]
    first = scalars[1] == 0
    squares = jnp.sum(total[0:1, 0:1], keepdims=True)
    norm = jnp.sqrt(squares)
    outs[27][...] = norm
    outs[28][...] = total[0:1, 1:2]
    factor = jnp.minimum(1.0, CLIP / (norm + 1e-06))

    def half_of(half, start, rows):
        here, there = kept[start : start + rows, :], got[start : start + rows, :]
        return jnp.where(first == (half == 0), here, there)

    def apply(index, spot, grad, rate, decay):
        results = adam_step(
            ins[index][spot], grad, ins[9 + index][spot], ins[18 + index][spot], rate, decay, factor
        )
        for which, result in enumerate(results):
            outs[9 * which + index][spot] = result

    for half in range(2):
        rows = slice(16 * half, 16 * half + 16)
        for u in range(3):
            apply(0, (0, rows, slice(D * u, D * (u + 1))), half_of(half, 16 * u, 16), 0.03, 0.01)
        apply(1, (0, rows, slice(None)), half_of(half, 192, 16), 0.03, 0.01)
        apply(2, (0, rows, slice(None)), half_of(half, 48, 16), 0.03, 0.01)
        for u in range(4):
            apply(3, (0, rows, slice(D * u, D * (u + 1))), half_of(half, 64 + 16 * u, 16), 0.03, 0.01)
        apply(4, (0, slice(64 * half, 64 * half + 64), slice(None)), half_of(half, 128, 64), 0.03, 0.01)
        for u in range(2):
            apply(7, (rows, slice(D * u, D * (u + 1))), half_of(half, 208 + 16 * u, 16), 0.03, 0.01)
        small[rows, :] = half_of(half, 240, 16)[:, 0:BLOCK]
    small[32:, :] = jnp.zeros((BLOCK - 32, BLOCK), F32)
    turned = jnp.transpose(small[...])
    apply(6, (slice(None), slice(None)), small[0:32, 0:FEATS], 0.03, 0.01)
    vecs = jnp.where(first, turned[80:84, 0:32], turned[84:88, 0:32])
    apply(5, (0, slice(None), slice(None)), vecs, 0.3, 0.0)
    apply(8, (slice(None), slice(None)), turned[88:89, 0:32], 0.3, 0.0)


def pack_shards(scalars, attn, out, pos, up, down, vecs, w_in, head, gain, kept, sent, codes, small):
    half, section = scalars[1], scalars[3]
    small[...] = jnp.zeros_like(small)
    small[88:89, 0:32] = gain[...]
    small[pl.ds(FEATS + 4 * section, 4), 0:32] = vecs[0]
    turned = jnp.transpose(small[...])[0:32]
    turned = jnp.concatenate([w_in[...], turned[:, FEATS:]], 1)
    column = lax.broadcasted_iota(jnp.int32, turned.shape, 1)
    shared = (column < FEATS) | (column == 88)
    for which, target in ((half, kept), (1 - half, sent)):
        rows = pl.ds(pl.multiple_of(16 * which, 16), 16)
        for u in range(3):
            target[16 * u : 16 * u + 16, :] = attn[0, rows, D * u : D * (u + 1)].astype(BF16)
        target[48:64, :] = pos[0, rows, :].astype(BF16)
        for u in range(4):
            target[80 + 16 * u : 96 + 16 * u, :] = up[0, rows, D * u : D * (u + 1)].astype(BF16)
        target[144:208, :] = down[0, pl.ds(pl.multiple_of(64 * which, 64), 64), :].astype(BF16)
        target[208:224, :] = out[0, rows, :].astype(BF16)
        tail = jnp.where(half == 0, turned[0:16], turned[16:32])
        if target is sent:
            tail = jnp.where(half == 0, turned[16:32], turned[0:16])
            tail = jnp.where(shared[0:16], 0.0, tail)
        target[64:80, :] = jnp.zeros((16, D), BF16)
        target[64:80, 0:BLOCK] = tail.astype(BF16)
    rows = pl.ds(pl.multiple_of(16 * half, 16), 16)
    for u in range(2):
        codes[16 * u : 16 * u + 16, :] = head[rows, D * u : D * (u + 1)].astype(BF16)


VMEM = pl.BlockSpec(memory_space=pltpu.VMEM)
ANY = pl.BlockSpec(memory_space=pl.ANY)
HBM = pl.BlockSpec(memory_space=pltpu.HBM)
SMEM = pl.BlockSpec(memory_space=pltpu.SMEM)
DMA = pltpu.SemaphoreType.DMA


def shape(*dims, dtype=F32):
    return jax.ShapeDtypeStruct(dims, dtype)


def half_shape(*dims):
    return jax.ShapeDtypeStruct(dims, BF16)


def held(*dims):
    return pltpu.VMEM(dims, BF16)


def wide(*dims):
    return pltpu.VMEM(dims, F32)


def call(body, name, ins, outs, out_specs, scratch, micros, limit):
    return pl.pallas_call(
        body,
        name=name,
        in_specs=ins,
        out_shape=outs,
        out_specs=out_specs,
        scratch_shapes=scratch,
        compiler_params=pltpu.CompilerParams(vmem_limit_bytes=limit * 1024 * 1024),
        cost_estimate=pl.CostEstimate(flops=micros * 1_150_000_000, bytes_accessed=1 << 20, transcendentals=0),
    )


QUERY_KEY = (half_shape(SEG, D), half_shape(SEG, D), half_shape(ROWS, D), half_shape(ROWS, D), half_shape(ROWS, D))
PROJECT_HELD = [held(ROWS, D), held(4, D, D), DMA, DMA((12,))]
KEPT = half_shape(KEPT_ROWS, D)


def run_project_first(bits, scalars, frames, pieces, table):
    result = call(
        functools.partial(project, bits, 0),
        "project_first",
        [SMEM, VMEM, HBM, HBM, HBM, HBM, VMEM],
        QUERY_KEY + (shape(SEG, D), shape(16, D), KEPT),
        [VMEM] * 7 + [HBM],
        PROJECT_HELD + [wide(ROWS, D), held(D, BLOCK), DMA],
        6,
        40,
    )(scalars, frames, *pieces, table)
    return result[:5], result[5], result[6], result[7]


def run_project(bits, scalars, memory, hidden, vecs, pieces, table):
    result = call(
        functools.partial(project, bits, 4),
        "project",
        [SMEM, VMEM, VMEM, VMEM, HBM, HBM, HBM, HBM, VMEM],
        QUERY_KEY + (KEPT,),
        [VMEM] * 5 + [HBM],
        PROJECT_HELD,
        6,
        40,
    )(scalars, memory, hidden, vecs, *pieces, table)
    return result[:5], result[5]


def run_attend(scalars, projected):
    return call(
        attend,
        "attend",
        [SMEM] + [VMEM] * 5,
        (half_shape(SEG, D), half_shape(KEPT_PAIRS, 2 * BLOCK, WIDE)),
        [VMEM, HBM],
        [held(PAIRS, 2 * BLOCK, WIDE), DMA((PAIRS + 2,))],
        11,
        44,
    )(scalars, *projected)


HALF_HELD = [
    held(SEG, 256), held(SEG, 256), held(ROWS, 256), held(ROWS, 256), held(ROWS, 256),
    held(2, 2 * BLOCK, WIDE), held(2 * BLOCK, 2 * BLOCK),
    wide(256, ROWS), wide(256, ROWS), wide(256, ROWS), wide(SEG, 256), wide(SEG, 256), DMA((2, 6)),
]
LATE_HELD = [held(ROWS, D), held(ROWS, D), DMA((2,))]
HALF_OUT = (half_shape(SEG, 256), half_shape(ROWS, 256), half_shape(ROWS, 256))


def run_attend_back(bits, scalars, grad_att, saved, table, probs):
    result = call(
        functools.partial(attend_back, bits, False),
        "attend_back",
        [SMEM, VMEM] + [HBM] * 3,
        HALF_OUT + (half_shape(4, D, 256), shape(8, 256)),
        [VMEM] * 5,
        HALF_HELD + LATE_HELD,
        9,
        40,
    )(scalars, grad_att, table, saved, probs)
    return (*result[:3], result[4]), result[3]


def run_attend_back_rest(bits, scalars, grad_att, saved, table, probs, staged):
    result = call(
        functools.partial(attend_back, bits, True),
        "attend_back_rest",
        [SMEM, VMEM] + [HBM] * 3 + [VMEM],
        HALF_OUT + (shape(8, 256), half_shape(GROUPS, 64, D), half_shape(GROUPS, 64, D)),
        [VMEM] * 4 + [ANY] * 2,
        HALF_HELD + [held(4, D, D), DMA] + LATE_HELD,
        10,
        42,
    )(scalars, grad_att, table, saved, probs, staged)
    return result[:4], result[4], result[5]


def run_input_grads(bits, scalars, saved, grads, grad_mixed, vecs, memory, hidden):
    return call(
        functools.partial(input_grads, bits, 4),
        "input_grads",
        [SMEM, HBM] + [VMEM] * 12,
        (shape(SEG, D), shape(8, D)),
        [VMEM] * 2,
        [held(4, D, D), DMA((3,))],
        5,
        50,
    )(scalars, saved, *grads, grad_mixed, vecs, memory, hidden)


def run_input_grads_last(bits, scalars, saved, grads, grad_mixed, vecs, frames, *small_grads):
    return call(
        functools.partial(input_grads, bits, 0),
        "input_grads_last",
        [SMEM, HBM] + [VMEM] * 15,
        (half_shape(GROUPS, 16, D), half_shape(GROUPS, 16, D)),
        [ANY] * 2,
        [wide(ROWS, D), wide(BLOCK, D), held(D, D), DMA, held(D, BLOCK), DMA, held(4, D, D), DMA((3,))],
        5,
        50,
    )(scalars, saved, *grads, grad_mixed, vecs, frames, *small_grads)


FEED_HELD = [held(SEG, D), held(SEG, FF), held(SEG, FF), held(D, FF), held(FF, D), held(D, D)]
BACK_HELD = [held(SEG, FF), held(D, FF), held(FF, D), held(D, D)]


def run_feed_forward(bits, base, scalars, residual, attended, vecs, pieces):
    result = call(
        functools.partial(feed_forward, bits, base),
        "feed_forward",
        [SMEM, VMEM, VMEM, VMEM, HBM, HBM, HBM, HBM],
        (shape(SEG, D), shape(MEM, D), shape(SEG, D), KEPT),
        [VMEM] * 2 + [HBM] * 2,
        [wide(SEG, D)] + FEED_HELD + [DMA((3,)), DMA((16,))],
        9,
        50,
    )(scalars, residual, attended, vecs, *pieces)
    return result


def run_feed_backward(bits, base, scalars, grad_out, vecs, mixed, probs, saved):
    return call(
        functools.partial(feed_backward, bits, base),
        "feed_backward",
        [SMEM, VMEM, VMEM] + [HBM] * 3,
        (half_shape(GROUPS, 144, D), half_shape(GROUPS, 144, D), shape(SEG, D), half_shape(SEG, D), shape(8, D)),
        [ANY, ANY, VMEM, VMEM, VMEM],
        [wide(SEG, D), held(SEG, D)] + FEED_HELD + BACK_HELD + [DMA((18,)), DMA((3,))],
        13,
        50,
    )(scalars, grad_out, vecs, mixed, probs, saved)


def run_top(bits, streams, scalars, residual, attended, targets, vecs, pieces):
    return call(
        functools.partial(top_kernel, bits, streams),
        "top_kernel",
        [SMEM, VMEM, VMEM, VMEM, VMEM, HBM, HBM, HBM, HBM],
        (
            half_shape(GROUPS, 176, D), half_shape(GROUPS, 176, D),
            shape(SEG, D), half_shape(SEG, D), shape(8, D), shape(8, D), shape(8, 128),
        ),
        [ANY] * 2 + [VMEM] * 5,
        FEED_HELD
        + [wide(SEG, D), wide(SEG, D), wide(SEG, D), held(D, CODES), held(SEG, D), held(SEG, CODES), held(D, CODES)]
        + BACK_HELD
        + [DMA, DMA((3,)), DMA((3,))],
        21,
        56,
    )(scalars, residual, attended, targets, vecs, *pieces)


def run_finish(scalars, loss, *sums):
    counts = tuple((len(item) for item in sums))
    flat = [item for group in sums for item in group]
    return call(
        functools.partial(finish, counts),
        "finish",
        [SMEM, VMEM] + [ANY] * len(flat),
        (shape(256, D), shape(256, D), shape(8, 128)),
        [VMEM] * 3,
        [pltpu.VMEM(item.shape[1:], item.dtype) for item in flat] + [DMA((len(flat),))],
        3,
        56,
    )(scalars, loss, *flat)


def run_update(scalars, total, kept, got, state):
    flat = [item[None] if item.ndim == 1 else item for item in state]
    for index in (6, 15, 24):
        flat[index] = jnp.transpose(flat[index])
    result = call(
        update,
        "update",
        [SMEM] + [VMEM] * 30,
        tuple((shape(*item.shape) for item in flat)) + (shape(1, 1), shape(1, 1)),
        [VMEM] * 29,
        [wide(BLOCK, BLOCK)],
        5,
        24,
    )(scalars, total, kept, got, *flat)
    result = list(result)
    for index in (6, 15, 24):
        result[index] = jnp.transpose(result[index])
    return [item.reshape(old.shape) for item, old in zip(result, state)] + [result[27][0, 0], result[28][0, 0]]


def run_pack(scalars, w_attn, w_out, w_pos, w_up, w_down, layer_vecs, w_in, w_head, gain_final):
    return call(
        pack_shards,
        "pack_shards",
        [SMEM] + [VMEM] * 9,
        (half_shape(224, D), half_shape(224, D), half_shape(32, D)),
        [VMEM] * 3,
        [wide(BLOCK, BLOCK)],
        3,
        56,
    )(scalars, w_attn, w_out, w_pos, w_up, w_down, layer_vecs, jnp.transpose(w_in), w_head, gain_final[None])


def spread(value, bits):
    count = lax.axis_size("dp")
    pairs = [
        (half * count + i, half * count + (i ^ bit)) for half, bit in enumerate(bits) for i in range(count)
    ]
    return lax.ppermute(value, ("section", "dp"), pairs)


def swap(value):
    return lax.ppermute(value, "section", [(0, 1), (1, 0)])


def fence(*values):
    return lax.optimization_barrier(values)


def joined(low, got):
    return jnp.concatenate([low, got], 0)


def part(sources, first, last):
    total = sources[0][first:last].astype(F32)
    for item in sources[1:]:
        total = total + item[first:last].astype(F32)
    return total


def shrink(chunks, pair, merged=()):
    count = (merged or chunks[0])[-1].shape[0]
    sent, first = [], 0
    for item in chunks:
        rows = item[0].shape[1]
        total = part(item, count // 2, count)
        if merged:
            total = total + part([other[:, first : first + rows] for other in merged], count // 2, count)
        sent.append(total.astype(BF16))
        first += rows
    return spread(jnp.concatenate(sent, 1), pair)


def add_up(value, bits):
    value = value + swap(value)
    steps = [low for low, unused in zip(*bits)]
    for one, two in zip(steps[0::2], steps[1::2]):
        first, second, third = (spread(value, (step, step)) for step in (one, two, one + two))
        value = (value + first) + (second + third)
    return value


def lanes_of(block):
    return [block[:, D * u : D * (u + 1)] for u in range(block.shape[1] // D)]


def sinus_table(where_at):
    freqs = jnp.exp(-jnp.log(10000.0) * (2.0 * jnp.arange(D // 2, dtype=jnp.int32).astype(F32) / D))
    angles = where_at * freqs[None, :]
    return jnp.concatenate([jnp.sin(angles), jnp.cos(angles)], 1).astype(BF16)


def split_shards(section, scalars, params):
    kept, sent, head = run_pack(scalars, *params)
    got = swap(sent)
    first = section == 0
    row = lax.broadcasted_iota(jnp.int32, (80, D), 0)
    attn = jnp.where(row < 64, jnp.where(first, kept[:80], got[:80]), kept[:80] + got[:80])
    zero = jnp.where(first, kept[80:], got[80:])
    one = jnp.where(first, got, kept)
    return attn, zero, one[:64], jnp.concatenate([one[80:], head], 0)


def halves(whole, rows):
    return whole.reshape(GROUPS, 2, rows, whole.shape[1]).transpose(1, 0, 2, 3)


def gather_whole(section, w_attn, w_out, w_pos, w_up, w_down, layer_vecs, w_in, w_head, gain_final):
    def over(value, axis):
        return lax.all_gather(value.astype(BF16), "dp", axis=axis, tiled=True)

    def layers(value):
        return lax.all_gather(over(value[0], 0), "section", axis=0)

    attn, out, pos, up, down = (layers(item) for item in (w_attn, w_out, w_pos, w_up, w_down))
    vecs = lax.all_gather(over(layer_vecs[0], 1), "section", axis=0)
    small = jnp.concatenate(
        [over(w_in, 1), vecs[0], vecs[1], over(gain_final, 0)[None], jnp.zeros((BLOCK - 89, D), BF16)], 0
    )
    small = jnp.pad(jnp.transpose(small), ((0, 0), (0, D - BLOCK)))
    head = over(w_head, 0)

    def pieces(units):
        both = jnp.concatenate([halves(item, item.shape[0] // 32) for item in units], 2)
        own = lax.dynamic_index_in_dim(both, section, 0, keepdims=False)
        other = lax.dynamic_index_in_dim(both, 1 - section, 0, keepdims=False)
        return (own[:8], own[8:], other[:8], other[8:])

    return (
        pieces(lanes_of(attn[0]) + [pos[0], small]),
        pieces(lanes_of(up[0]) + [down[0], out[0]]),
        pieces(lanes_of(attn[1]) + [pos[1]]),
        pieces(lanes_of(up[1]) + [down[1], out[1]] + lanes_of(head)),
    )


def whole_grads(section, sums):
    count = lax.axis_size("dp")
    place = lax.axis_index("dp")
    attn_zero, feed_zero, attn_one, feed_one, small = (
        lax.all_gather(lax.psum(item, "dp"), "section", axis=0) for item in sums
    )

    def unit(both, start, rows):
        item = both[:, :, start : start + rows]
        return item.transpose(1, 0, 2, 3).reshape(GROUPS * 2 * rows, both.shape[3])

    def layer(attn, feed):
        return (
            jnp.concatenate([unit(attn, 16 * u, 16) for u in range(3)], 1),
            unit(feed, 128, 16),
            unit(attn, 48, 16),
            jnp.concatenate([unit(feed, 16 * u, 16) for u in range(4)], 1),
            unit(feed, 64, 64),
        )

    small = jnp.transpose(unit(small, 0, 16))
    zero = layer(attn_zero, feed_zero) + (small[80:84],)
    one = layer(attn_one, feed_one) + (small[84:88],)
    ends = (small[:80], jnp.concatenate([unit(feed_one, 144 + 16 * u, 16) for u in range(2)], 1), small[88])
    squares = sum((jnp.sum(item * item) for item in zero + one + ends))
    dims = (0, 0, 0, 0, 0, 1, 1, 0, 0)
    grads = tuple((jnp.where(section == 0, a, b) for a, b in zip(zero, one))) + ends
    return squares, tuple(
        (
            lax.dynamic_slice_in_dim(item, place * (item.shape[dim] // count), item.shape[dim] // count, dim)
            for item, dim in zip(grads, dims)
        )
    )


def local(frames, targets, lengths, *state):
    params, firsts, seconds = (state[:9], state[9:18], state[18:])
    section = lax.axis_index("section")
    streams = lax.axis_size("dp")
    ringed = streams == GROUPS
    place = lax.axis_index("dp") if ringed else jnp.int32(0)
    length = lengths[0]
    scalars = jnp.stack([place, section, length, section]).astype(jnp.int32)
    count_down = (ROWS - 1 - jnp.arange(ROWS, dtype=jnp.int32)).astype(F32)[:, None]
    rows = lax.dynamic_slice_in_dim(
        jnp.pad(frames[0], ((MEM, 0), (0, BLOCK - FEATS))), section * SEG, ROWS, 0
    )
    codes = lax.dynamic_slice_in_dim(targets, section * SEG, SEG, 1)
    if ringed:
        bits = ((8, 4, 1, 2), (8, 4, 2, 1))
        far, near, side, last = zip(*bits)
        zero, one, two, three = (item[None] for item in split_shards(section, scalars, params))
        zero, got, count_down = fence(zero, spread(zero, far), count_down)
        table = sinus_table(count_down)
        zero = joined(zero, got)
        zero, got, one = fence(zero, spread(zero, near), one)
        zero = joined(zero, got)
        one_got = spread(one, far)
        zero, got, two, one, one_got, rows, table, codes = fence(
            zero, spread(zero, side), two, one, one_got, rows, table, codes
        )
        zero = joined(zero, got)
        high = spread(zero, last)
        one = joined(one, one_got)
        one_got, two_got = spread(one, near), spread(two, far)
        zero, high, one, one_got, two, two_got = fence(zero, high, one, one_got, two, two_got)
        one, two = joined(one, one_got), joined(two, two_got)
        one_got, two_got = spread(one, side), spread(two, near)
        swapped, high_swapped = swap(zero), swap(high)
        swapped, high_swapped, one, one_got, two, two_got, three = fence(
            swapped, high_swapped, one, one_got, two, two_got, three
        )
        chunk = (zero, high, swapped, high_swapped)
        one, two = joined(one, one_got), joined(two, two_got)
        one_got, two_got, three_got, swapped = spread(one, last), spread(two, side), spread(three, far), swap(one)
    else:
        bits = IN_ORDER
        table = sinus_table(count_down)
        chunk, chunk_one, chunk_two, chunk_three = gather_whole(section, *params)

    projected, hidden_zero, vecs, saved_zero = run_project_first(bits, scalars, rows, chunk, table)
    if ringed:
        projected, two_got, three_got, swapped = fence(projected, two_got, three_got, swapped)
        two, three = joined(two, two_got), joined(three, three_got)
        two_got, three_got, two_swapped = spread(two, last), spread(three, near), swap(two)
    attended, probs_zero = run_attend(scalars, projected)
    if ringed:
        attended, one_got, two_got, three_got, two_swapped = fence(
            attended, one_got, two_got, three_got, two_swapped
        )
        chunk = (one, one_got, swapped, swap(one_got))
        two_chunk = (two, two_got, two_swapped, swap(two_got))
        three = joined(three, three_got)
        three_got = spread(three, side)
    else:
        chunk = chunk_one
    out_zero, memory, mixed_zero, fed_zero = run_feed_forward(bits, 0, scalars, hidden_zero, attended, vecs, chunk)
    if ringed:
        out_zero, memory, three_got, two_chunk = fence(out_zero, memory, three_got, two_chunk)
        chunk = two_chunk
        three = joined(three, three_got)
        three_got, three_swapped = spread(three, last), swap(three)
    else:
        chunk = chunk_two
    memory = lax.ppermute(memory, "section", [(0, 1)])
    projected, saved_one = run_project(bits, scalars, memory, out_zero, vecs, chunk, table)
    attended, probs_one = run_attend(scalars, projected)
    if ringed:
        attended, three_got, three_swapped = fence(attended, three_got, three_swapped)
        chunk = (three, three_got, three_swapped, swap(three_got))
    else:
        chunk = chunk_three
    keep_a, send_a, grad, grad_att, gain_one, gain_final, loss = run_top(
        bits, streams, scalars, out_zero, attended, codes, vecs, chunk
    )
    if ringed:
        grad_att, keep_a, send_a = fence(grad_att, keep_a, send_a)
        got_a = swap(send_a)
    grads_a, staged = run_attend_back(bits, scalars, grad_att, saved_one, table, probs_one)
    if ringed:
        grads_a, staged, got_a = fence(grads_a, staged, got_a)
        sum_a = [keep_a, got_a]
        got_a = shrink([sum_a], last)
    grads_b, keep_b, send_b = run_attend_back_rest(
        bits, scalars, grad_att, saved_one, table, probs_one, staged
    )
    if ringed:
        grads_b, keep_b, send_b = fence(grads_b, keep_b, send_b)
        got_b = swap(send_b)
    grad, vecs_one = run_input_grads(
        bits, scalars, saved_one, (*grads_a, *grads_b), grad, vecs, memory, out_zero
    )
    if ringed:
        grad, got_a, got_b = fence(grad, got_a, got_b)
        sum_a.append(got_a)
        sum_b = [keep_b, got_b]
        got_a, got_b = shrink([sum_a], side), shrink([sum_b], last)
    keep_c, send_c, grad, grad_att, gain_zero = run_feed_backward(
        bits, 0, scalars, grad, vecs, mixed_zero, probs_zero, fed_zero
    )
    if ringed:
        grad_att, got_a, got_b, keep_c, send_c = fence(grad_att, got_a, got_b, keep_c, send_c)
        sum_a.append(got_a)
        sum_b.append(got_b)
        got_a, got_b, got_c = shrink([sum_a], near), shrink([sum_b], side), swap(send_c)
    grads_a, staged = run_attend_back(bits, scalars, grad_att, saved_zero, table, probs_zero)
    if ringed:
        grads_a, staged, got_a, got_b, got_c = fence(grads_a, staged, got_a, got_b, got_c)
        sum_a.append(got_a)
        sum_b.append(got_b)
        sum_c = [keep_c, got_c]
        got_c, got_a, got_b = shrink([sum_c], last), shrink([sum_a], far), shrink([sum_b], near)
    grads_b, keep_d, send_d = run_attend_back_rest(
        bits, scalars, grad_att, saved_zero, table, probs_zero, staged
    )
    if ringed:
        grads_b, keep_d, send_d, got_a, got_b, got_c = fence(grads_b, keep_d, send_d, got_a, got_b, got_c)
        sum_a.append(got_a)
        sum_b.append(got_b)
        sum_c.append(got_c)
        got_d, got_c, got_b = swap(send_d), shrink([sum_c], side), shrink([sum_b], far)
    keep_e, send_e = run_input_grads_last(
        bits, scalars, saved_zero, (*grads_a, *grads_b), grad, vecs, rows,
        gain_zero, vecs_one, gain_one, gain_final,
    )
    if not ringed:
        pairs = ((keep_d, send_d), (keep_c, send_c), (keep_b, send_b), (keep_a, send_a), (keep_e, send_e))
        sums = [keep.astype(F32) + swap(send).astype(F32) for keep, send in pairs]
        squares, grads = whole_grads(section, sums)
        grad_norm = jnp.sqrt(squares)
        loss_sum = lax.psum(loss[0, 0], ("section", "dp"))
        factor = jnp.minimum(1.0, CLIP / (grad_norm + 1e-06))
        results = []
        for index in range(9):
            rate, decay = (0.3, 0.0) if index in (5, 8) else (0.03, 0.01)
            grad = grads[index][None] if index < 6 else grads[index]
            results.append(
                adam_step(params[index], grad, firsts[index], seconds[index], rate, decay, factor)
            )
        news, moms, sqs = zip(*results)
        return (*news, *moms, *sqs, grad_norm, loss_sum)
    keep_e, send_e, got_b, got_d = fence(keep_e, send_e, got_b, got_d)
    sum_b.append(got_b)
    sum_d, sum_e, sum_de = [keep_d, got_d], [keep_e, swap(send_e)], []
    for pair in (last, side, near, far):
        got = shrink([sum_d, sum_e], pair, sum_de)
        if pair == last:
            sum_c.append(got_c)
            got, got_c = fence(got, shrink([sum_c], near))
            sum_c.append(got_c)
            sum_c.append(shrink([sum_c], far))
        sum_de.append(got)
    kept, sent, total = run_finish(scalars, loss, sum_d, sum_c, sum_b, sum_a, sum_e, sum_de)
    got = swap(sent)
    return tuple(run_update(scalars, add_up(total, bits), kept, got, state))


def solution(mesh):
    weights = (
        P("section", "dp", None),
        P("section", "dp", None),
        P("section", "dp", None),
        P("section", "dp", None),
        P("section", "dp", None),
        P("section", None, "dp"),
        P(None, "dp"),
        P("dp", None),
        P("dp"),
    )
    return jax.shard_map(
        local,
        mesh=mesh,
        in_specs=(P("dp", None, None), P("dp", None), P("dp")) + weights * 3,
        out_specs=weights * 3 + (P(), P()),
        check_vma=False,
    )
```

profile of v0, /device:TPU:0, one launch (start us, length us, event | category | flops | bytes accessed | tf_op | source)
XLA Modules:
  0.0 292.5 jit_solution(12381292709960600714)
XLA Ops:
  1.9 2.2 pack_shards.1
  6.9 4.0 %collective-permute-start.1 = (bf16[1,80,512]{2,1,0:T(8,128)(2,1)S(1)}, bf16[1,80,512]{2,1,0:T(8,128)(2,1)S(1)}, u32[]{:S(2)}, u32[]{:S(2)}) collective-permute-start(bf16[1,80,512]{2,1,0:T(8,128)(2,1)S(1)} %select_bitcast_fusion), channel_id=1, source_target_pairs={{0,8},{1,9},{2,10},{3,11},{4,12},{5,13},{6,14},{7,15},{8,0},{9,1},... | collective-permute-start | bytes 245768 | tf_op jit(solution)/shard_map/ppermute | solution.py:990
  10.9 4.4 %collective-permute-done.1 = bf16[1,80,512]{2,1,0:T(8,128)(2,1)S(1)} collective-permute-done((bf16[1,80,512]{2,1,0:T(8,128)(2,1)S(1)}, bf16[1,80,512]{2,1,0:T(8,128)(2,1)S(1)}, u32[]{:S(2)}, u32[]{:S(2)}) %collective-permute-start.1) | collective-permute-done | bytes 81952 | tf_op jit(solution)/shard_map/ppermute | solution.py:990
  16.2 5.0 %collective-permute-done.2 = bf16[2,80,512]{2,1,0:T(8,128)(2,1)S(1)} collective-permute-done((bf16[2,80,512]{2,1,0:T(8,128)(2,1)S(1)}, bf16[2,80,512]{2,1,0:T(8,128)(2,1)S(1)}, u32[]{:S(2)}, u32[]{:S(2)}) %collective-permute-start.2) | collective-permute-done | bytes 163872 | tf_op jit(solution)/shard_map/ppermute | solution.py:990
  21.2 2.8 collective-permute-start.4
  24.0 1.6 collective-permute-start.3
  25.6 3.2 %fusion = (bf16[768,256]{1,0:T(8,128)(2,1)S(1)}, bf16[768,256]{1,0:T(8,128)(2,1)S(1)}) fusion(f32[256]{0:T(256)S(1)} %multiply_exponential_fusion, f32[768]{0:T(1024)S(1)} %reduce), kind=kLoop, calls=%fused_computation.8 | loop fusion | flops 589824 | bytes 790528 | tf_op jit(solution)/shard_map/convert
  28.8 1.8 collective-permute-done.4
  31.2 1.6 collective-permute-start.5
  32.8 1.8 collective-permute-start.6
  34.6 1.8 collective-permute-start.7
  36.5 4.1 %collective-permute-done.7 = bf16[1,64,512]{2,1,0:T(8,128)(2,1)S(1)} collective-permute-done((bf16[1,64,512]{2,1,0:T(8,128)(2,1)S(1)}, bf16[1,64,512]{2,1,0:T(8,128)(2,1)S(1)}, u32[]{:S(2)}, u32[]{:S(2)}) %collective-permute-start.7) | collective-permute-done | bytes 65568 | tf_op jit(solution)/shard_map/ppermute | solution.py:990
  42.5 1.6 collective-permute-start.10
  44.1 2.0 collective-permute-start.11
  46.1 4.4 %collective-permute-done.11 = bf16[2,64,512]{2,1,0:T(8,128)(2,1)S(1)} collective-permute-done((bf16[2,64,512]{2,1,0:T(8,128)(2,1)S(1)}, bf16[2,64,512]{2,1,0:T(8,128)(2,1)S(1)}, u32[]{:S(2)}, u32[]{:S(2)}) %collective-permute-start.11) | collective-permute-done | bytes 131104 | tf_op jit(solution)/shard_map/ppermute | solution.py:990
  50.5 2.0 collective-permute-done.10
  52.6 1.6 collective-permute-start.15
  54.2 2.1 collective-permute-start.13
  57.0 6.7 %project_first.1 = (bf16[512,512]{1,0:T(8,128)(2,1)S(1)}, bf16[512,512]{1,0:T(8,128)(2,1)S(1)}, bf16[768,512]{1,0:T(8,128)(2,1)S(1)}, bf16[768,512]{1,0:T(8,128)...) custom-call(s32[4]{0:T(128)S(1)} %copy-done.8, ...), custom_call_target="tpu_custom_call" | custom-call | flops 6899999744 | bytes 1048576 | tf_op jit(solution)/shard_map/project_first/pallas_call | solution.py:784
  67.0 1.9 collective-permute-start.17
  68.9 6.1 %attend.2 = (bf16[512,512]{1,0:T(8,128)(2,1)S(1)}, bf16[14,256,2304]{2,1,0:T(8,128)(2,1)}) custom-call(s32[4]{0:T(128)S(1)} %copy-done.8, bf16[512,512]{1,0:T(8,128)(2,1)S(1)} %get-tuple-element.249.query_u, bf16[512,512]{1,0:T(8,128)(2,1)S(1)} %get-tuple-element.250.query_v, bf16[768,512]{1,0:T(8,128)(2,1)S(1)} %get-tuple-element.251.keys, ...), custom_call_target="tpu_custom_call" | custom-call | flops 12650000384 | bytes 1048576 | tf_op jit(solution)/shard_map/attend/pallas_call | solution.py:812
  75.1 2.6 collective-permute-done.17
  78.8 1.5 collective-permute-start.20
  82.1 9.3 %feed_forward.1 = (f32[512,512]{1,0:T(8,128)S(1)}, f32[256,512]{1,0:T(8,128)S(1)}, f32[512,512]{1,0:T(8,128)S(1)}, bf16[16384,512]{1,0:T(8,128)(2,1)}) custom-call(s32[4]{0:T(128)S(1)} %copy-done.8, f32[512,512]{1,0:T(8,128)} %copy-done.42, bf16[512,512]{1,0:T(8,128)(2,1)S(1)} %get-tuple-element.257.attended, ...), custom_call_target="tpu_custom_call" | custom-call | flops 10350000128 | bytes 1048576 | tf_op jit(solution)/shard_map/feed_forward/pallas_call | solution.py:892
  91.5 2.3 collective-permute-start.22
  95.3 6.3 %project.1 = (bf16[512,512]{1,0:T(8,128)(2,1)S(1)}, bf16[512,512]{1,0:T(8,128)(2,1)S(1)}, bf16[768,512]{1,0:T(8,128)(2,1)S(1)}, bf16[768,512]{1,0:T(8,128)(2,1)S...) custom-call(s32[4]{0:T(128)S(1)} %copy-done.8, f32[256,512]{1,0:T(8,128)S(1)} %collective-permute-done.22.refs_1_.refs_12_, ...), custom_call_target="tpu_custom_call" | custom-call | flops 6899999744 | bytes 1048576 | tf_op jit(solution)/shard_map/project/pallas_call | solution.py:798
  101.6 14.2 %attend.3 = (bf16[512,512]{1,0:T(8,128)(2,1)S(1)}, bf16[14,256,2304]{2,1,0:T(8,128)(2,1)}) custom-call(s32[4]{0:T(128)S(1)} %copy-done.8, bf16[512,512]{1,0:T(8,128)(2,1)S(1)} %get-tuple-element.272.query_u, bf16[512,512]{1,0:T(8,128)(2,1)S(1)} %get-tuple-element.273.query_v, bf16[768,512]{1,0:T(8,128)(2,1)S(1)} %get-tuple-element.274.keys, ...), custom_call_target="tpu_custom_call" | custom-call | flops 12650000384 | bytes 1048576 | tf_op jit(solution)/shard_map/attend/pallas_call | solution.py:812
  117.7 4.0 %collective-permute-start.25 = (bf16[8,176,512]{2,1,0:T(8,128)(2,1)S(1)}, bf16[8,176,512]{2,1,0:T(8,128)(2,1)S(1)}, u32[]{:S(2)}, u32[]{:S(2)}) collective-permute-start(bf16[8,176,512]{2,1,0:T(8,128)(2,1)S(1)} %collective-permute-done.23.own_high), channel_id=1, source_target_pairs={{0,16},{16,0},{1,17},{17,1},{2,18},{18,2},{3,19},{19,3},{4,20},{20... | collective-permute-start | bytes 4325384 | tf_op jit(solution)/shard_map/ppermute | solution.py:994
  121.8 2.8 collective-permute-done.25.other_high
  125.8 18.2 %top_kernel.1 = (bf16[16,176,512]{2,1,0:T(8,128)(2,1)}, bf16[16,176,512]{2,1,0:T(8,128)(2,1)}, f32[512,512]{1,0:T(8,128)}, bf16[512,512]{1,0:T(8,128)(2,1)}, f32...) custom-call(s32[4]{0:T(128)} %pad_add_fusion.scalars.refs_0_, f32[512,512]{1,0:T(8,128)} %copy-done.4, ...), custom_call_target="tpu_custom_call" | custom-call | flops 24149999616 | bytes 1048576 | tf_op jit(solution)/shard_map/top_kernel/pallas_call | solution.py:919
  145.5 6.7 %attend_back.2 = (bf16[512,256]{1,0:T(8,128)(2,1)S(1)}, bf16[768,256]{1,0:T(8,128)(2,1)S(1)}, bf16[768,256]{1,0:T(8,128)(2,1)S(1)}, bf16[4,512,256]{2,1,0:T(8,128)(2,1)S(1)}, f32[8,256]{1,0:T(8,128)S(1)}) custom-call(s32[4]{0:T(128)S(1)} %copy-done.9, bf16[512,512]{1,0:T(8,128)(2,1)S(1)} %copy-done.39, ...), custom_call_target="tpu_custom_call" | custom-call | flops 10350000128 | bytes 1048576 | tf_op jit(solution)/shard_map/attend_back/pallas_call | solution.py:834
  152.3 1.9 add_convert_fusion
  154.7 9.7 %attend_back_rest.2 = (bf16[512,256]{1,0:T(8,128)(2,1)S(1)}, bf16[768,256]{1,0:T(8,128)(2,1)S(1)}, bf16[768,256]{1,0:T(8,128)(2,1)S(1)}, f32[8,256]{1,0:T(8,128)...) custom-call(s32[4]{0:T(128)S(1)} %copy-done.9, bf16[512,512]{1,0:T(8,128)(2,1)S(1)} %copy-done.39, ...), custom_call_target="tpu_custom_call" | custom-call | flops 11500000256 | bytes 1048576 | tf_op jit(solution)/shard_map/attend_back_rest/pallas_call | solution.py:848
  164.4 4.5 %collective-permute-start.28 = (bf16[16,64,512]{2,1,0:T(8,128)(2,1)S(1)}, bf16[16,64,512]{2,1,0:T(8,128)(2,1)}, u32[]{:S(2)}, u32[]{:S(2)}) collective-permute-start(bf16[16,64,512]{2,1,0:T(8,128)(2,1)S(1)} %get-tuple-element.309), channel_id=1, source_target_pairs={{0,16},{16,0},{1,17},{17,1},{2,18},{18,2},{3,19},{19,3},{4,20},{20... | collective-permute-start | bytes 3145736 | tf_op jit(solution)/shard_map/ppermute | solution.py:994
  168.9 4.5 %input_grads.1 = (f32[512,512]{1,0:T(8,128)S(1)}, f32[8,512]{1,0:T(8,128)S(1)}) custom-call(s32[4]{0:T(128)S(1)} %copy-done.9, bf16[16384,512]{1,0:T(8,128)(2,1)} %get-tuple-element.284.refs_3_.refs_1_, bf16[512,256]{1,0:T(8,128)(2,1)S(1)} %get-tuple-element.296.refs_2_, bf16[768,256]{1,0:T(8,128)(2,1)S(1)} %get-tuple-element.297.refs_3_, ...), custom_call_target="tpu_custom_call" | custom-call | flops 5750000128 | bytes 1048576 | tf_op jit(solution)/shard_map/input_grads/pallas_call | solution.py:862
  175.2 1.4 add_convert_fusion.2
  176.6 1.5 collective-permute-start.29
  178.1 11.1 %feed_backward.1 = (bf16[16,144,512]{2,1,0:T(8,128)(2,1)}, bf16[16,144,512]{2,1,0:T(8,128)(2,1)}, f32[512,512]{1,0:T(8,128)S(1)}, bf16[512,512]{1,0:T(8,128)(2,1)S(1)}, f32[8,512]{1,0:T(8,128)S(1)}) custom-call(s32[4]{0:T(128)S(1)} %copy-done.9, f32[512,512]{1,0:T(8,128)S(1)} %get-tuple-element.310.grad_out, f32[16,512]{1,0:T(8,128)S(1)} %copy-done.7, ...), custom_call_target="tpu_custom_call" | custom-call | flops 14949999616 | bytes 1048576 | tf_op jit(solution)/shard_map/feed_backward/pallas_call | solution.py:906
  189.2 2.3 collective-permute-done.29.refs_19_
  192.8 1.5 collective-permute-start.32
  196.4 6.6 %attend_back.3 = (bf16[512,256]{1,0:T(8,128)(2,1)S(1)}, bf16[768,256]{1,0:T(8,128)(2,1)S(1)}, bf16[768,256]{1,0:T(8,128)(2,1)S(1)}, bf16[4,512,256]{2,1,0:T(8,128)(2,1)S(1)}, f32[8,256]{1,0:T(8,128)S(1)}) custom-call(s32[4]{0:T(128)S(1)} %copy-done.9, bf16[512,512]{1,0:T(8,128)(2,1)S(1)} %get-tuple-element.320.refs_1_, ...), custom_call_target="tpu_custom_call" | custom-call | flops 10350000128 | bytes 1048576 | tf_op jit(solution)/shard_map/attend_back/pallas_call | solution.py:834
  203.0 2.8 collective-permute-done.31.refs_20_
  206.9 1.8 collective-permute-start.35
  210.7 1.8 collective-permute-start.34
  212.5 9.5 %attend_back_rest.3 = (bf16[512,256]{1,0:T(8,128)(2,1)S(1)}, bf16[768,256]{1,0:T(8,128)(2,1)S(1)}, bf16[768,256]{1,0:T(8,128)(2,1)S(1)}, f32[8,256]{1,0:T(8,128)...) custom-call(s32[4]{0:T(128)S(1)} %copy-done.9, ...), custom_call_target="tpu_custom_call" | custom-call | flops 11500000256 | bytes 1048576 | tf_op jit(solution)/shard_map/attend_back_rest/pallas_call | solution.py:848
  222.1 3.3 %collective-permute-done.36.refs_6_ = bf16[8,144,512]{2,1,0:T(8,128)(2,1)S(1)} collective-permute-done((bf16[8,144,512]{2,1,0:T(8,128)(2,1)S(1)}, bf16[8,144,512]{2,1,0:T(8,128)(2,1)S(1)}, u32[]{:S(2)}, u32[]{:S(2)}) %collective-permute-start.36) | collective-permute-done | bytes 1179680 | tf_op jit(solution)/shard_map/ppermute | solution.py:990
  226.5 1.8 collective-permute-start.37
  229.2 5.1 %input_grads_last.1 = (bf16[16,16,512]{2,1,0:T(8,128)(2,1)S(1)}, bf16[16,16,512]{2,1,0:T(8,128)(2,1)S(1)}) custom-call(s32[4]{0:T(128)S(1)} %copy-done.9, bf16[16384,512]{1,0:T(8,128)(2,1)} %get-tuple-element.321.refs_3_.refs_1_, bf16[512,256]{1,0:T(8,128)(2,1)S(1)} %get-tuple-element.342.refs_2_, bf16[768,256]{1,0:T(8,128)(2,1)S(1)} %get-tuple-element.343.refs_3_, ...), custom_call_target="tpu_custom_call" | custom-call | flops 5750000128 | bytes 1048576 | tf_op jit(solution)/shard_map/input_grads_last/pallas_call | solution.py:875
  234.6 1.4 collective-permute-done.40.refs_23_
  236.9 1.5 collective-permute-done.39.refs_7_
  238.4 1.4 add_convert_fusion.7
  240.2 7.8 %collective-permute-done.42.refs_8_ = bf16[2,144,512]{2,1,0:T(8,128)(2,1)S(1)} collective-permute-done((bf16[2,144,512]{2,1,0:T(8,128)(2,1)S(1)}, bf16[2,144,512]{2,1,0:T(8,128)(2,1)S(1)}, u32[]{:S(2)}, u32[]{:S(2)}) %collective-permute-start.42) | collective-permute-done | bytes 294944 | tf_op jit(solution)/shard_map/ppermute | solution.py:990
  248.9 6.5 %collective-permute-done.44.refs_25_ = bf16[4,80,512]{2,1,0:T(8,128)(2,1)S(1)} collective-permute-done((bf16[4,80,512]{2,1,0:T(8,128)(2,1)S(1)}, bf16[4,80,512]{2,1,0:T(8,128)(2,1)S(1)}, u32[]{:S(2)}, u32[]{:S(2)}) %collective-permute-start.44) | collective-permute-done | bytes 327712 | tf_op jit(solution)/shard_map/ppermute | solution.py:990
  256.9 1.3 collective-permute-start.43
  258.2 3.4 %collective-permute-done.45.refs_26_ = bf16[2,80,512]{2,1,0:T(8,128)(2,1)S(1)} collective-permute-done((bf16[2,80,512]{2,1,0:T(8,128)(2,1)S(1)}, bf16[2,80,512]{2,1,0:T(8,128)(2,1)S(1)}, u32[]{:S(2)}, u32[]{:S(2)}) %collective-permute-start.45) | collective-permute-done | bytes 163872 | tf_op jit(solution)/shard_map/ppermute | solution.py:990
  261.7 2.1 collective-permute-start.46
  263.8 2.9 %collective-permute-done.43.refs_9_ = bf16[1,144,512]{2,1,0:T(8,128)(2,1)S(1)} collective-permute-done((bf16[1,144,512]{2,1,0:T(8,128)(2,1)S(1)}, bf16[1,144,512]{2,1,0:T(8,128)(2,1)S(1)}, u32[]{:S(2)}, u32[]{:S(2)}) %collective-permute-start.43) | collective-permute-done | bytes 147488 | tf_op jit(solution)/shard_map/ppermute | solution.py:990
  268.5 4.5 %finish.1 = (f32[256,512]{1,0:T(8,128)}, f32[256,512]{1,0:T(8,128)}, f32[8,128]{1,0:T(8,128)}) custom-call(s32[4]{0:T(128)} %pad_add_fusion.scalars.refs_0_, f32[8,128]{1,0:T(8,128)} %get-tuple-element.283.refs_1_, bf16[16,64,512]{2,1,0:T(8,128)(2,1)} %copy-done.3, bf16[16,64,512]{2,1,0:T(8,128)(2,1)} %copy-done.49, ...), custom_call_target="tpu_custom_call" | custom-call | flops 3449999872 | bytes 1048576 | tf_op jit(solution)/shard_map/finish/pallas_call | solution.py:940
  273.6 1.6 collective-permute-done.47
  276.0 1.5 collective-permute-start.50
  278.0 2.3 collective-permute-start.48
  282.6 1.7 collective-permute-start.53
  284.8 1.3 collective-permute-start.51
  289.7 2.5 update.1
  (281 shorter events, 44.1 us)
Async XLA Ops:
  4.1 1.8 collective-permute-start
  6.9 8.5 %collective-permute-start.1 = (bf16[1,80,512]{2,1,0:T(8,128)(2,1)S(1)}, bf16[1,80,512]{2,1,0:T(8,128)(2,1)S(1)}, u32[]{:S(2)}, u32[]{:S(2)}) collective-permute-start(bf16[1,80,512]{2,1,0:T(8,128)(2,1)S(1)} %select_bitcast_fusion), channel_id=1, source_target_pairs={{0,8},{1,9},{2,10},{3,11},{4,12},{5,13},{6,14},{7,15},{8,0},{9,1},... | collective-permute-start | bytes 245768 | tf_op jit(solution)/shard_map/ppermute | solution.py:990
  15.4 5.8 %collective-permute-start.2 = (bf16[2,80,512]{2,1,0:T(8,128)(2,1)S(1)}, bf16[2,80,512]{2,1,0:T(8,128)(2,1)S(1)}, u32[]{:S(2)}, u32[]{:S(2)}) collective-permute-start(bf16[2,80,512]{2,1,0:T(8,128)(2,1)S(1)} %constant_dynamic-update-slice_fusion), channel_id=1, source_target_pairs={{0,4},{1,5},{2,6},{3,7},{4,0},{5,1},{6,2},{7,3},{8,12},{9,13},{10,... | collective-permute-start | bytes 491528 | tf_op jit(solution)/shard_map/ppermute | solution.py:990
  21.2 9.4 %collective-permute-start.4 = (bf16[1,144,512]{2,1,0:T(8,128)(2,1)S(1)}, bf16[1,144,512]{2,1,0:T(8,128)(2,1)S(1)}, u32[]{:S(2)}, u32[]{:S(2)}) collective-permute-start(bf16[1,144,512]{2,1,0:T(8,128)(2,1)S(1)} %fusion.2), channel_id=1, source_target_pairs={{0,8},{1,9},{2,10},{3,11},{4,12},{5,13},{6,14},{7,15},{8,0},{9,1},... | collective-permute-start | bytes 442376 | tf_op jit(solution)/shard_map/ppermute | solution.py:990
  24.0 7.1 %collective-permute-start.3 = (bf16[4,80,512]{2,1,0:T(8,128)(2,1)S(1)}, bf16[4,80,512]{2,1,0:T(8,128)(2,1)S(1)}, u32[]{:S(2)}, u32[]{:S(2)}) collective-permute-start(bf16[4,80,512]{2,1,0:T(8,128)(2,1)S(1)} %constant_dynamic-update-slice_fusion.2), channel_id=1, source_target_pairs={{0,1},{1,0},{2,3},{3,2},{4,5},{5,4},{6,7},{7,6},{8,9},{9,8},{10,11... | collective-permute-start | bytes 983048 | tf_op jit(solution)/shard_map/ppermute | solution.py:990
  31.2 10.7 %collective-permute-start.5 = (bf16[8,80,512]{2,1,0:T(8,128)(2,1)S(1)}, bf16[8,80,512]{2,1,0:T(8,128)(2,1)S(1)}, u32[]{:S(2)}, u32[]{:S(2)}) collective-permute-start(bf16[8,80,512]{2,1,0:T(8,128)(2,1)S(1)} %constant_dynamic-update-slice_fusion.4.refs_2_), channel_id=1, source_target_pairs={{0,2},{1,3},{2,0},{3,1},{4,6},{5,7},{6,4},{7,5},{8,10},{9,11},{10,... | collective-permute-start | bytes 1966088 | tf_op jit(solution)/shard_map/ppermute | solution.py:990
  32.8 8.7 %collective-permute-start.6 = (bf16[2,144,512]{2,1,0:T(8,128)(2,1)S(1)}, bf16[2,144,512]{2,1,0:T(8,128)(2,1)S(1)}, u32[]{:S(2)}, u32[]{:S(2)}) collective-permute-start(bf16[2,144,512]{2,1,0:T(8,128)(2,1)S(1)} %constant_dynamic-update-slice_fusion.6), channel_id=1, source_target_pairs={{0,4},{1,5},{2,6},{3,7},{4,0},{5,1},{6,2},{7,3},{8,12},{9,13},{10,... | collective-permute-start | bytes 884744 | tf_op jit(solution)/shard_map/ppermute | solution.py:990
  34.6 5.9 %collective-permute-start.7 = (bf16[1,64,512]{2,1,0:T(8,128)(2,1)S(1)}, bf16[1,64,512]{2,1,0:T(8,128)(2,1)S(1)}, u32[]{:S(2)}, u32[]{:S(2)}) collective-permute-start(bf16[1,64,512]{2,1,0:T(8,128)(2,1)S(1)} %slice_bitcast_fusion), channel_id=1, source_target_pairs={{0,8},{1,9},{2,10},{3,11},{4,12},{5,13},{6,14},{7,15},{8,0},{9,1},... | collective-permute-start | bytes 196616 | tf_op jit(solution)/shard_map/ppermute | solution.py:990
  41.9 10.6 %collective-permute-start.8 = (bf16[8,80,512]{2,1,0:T(8,128)(2,1)S(1)}, bf16[8,80,512]{2,1,0:T(8,128)(2,1)S(1)}, u32[]{:S(2)}, u32[]{:S(2)}) collective-permute-start(bf16[8,80,512]{2,1,0:T(8,128)(2,1)S(1)} %constant_dynamic-update-slice_fusion.4.refs_2_), channel_id=1, source_target_pairs={{0,16},{16,0},{1,17},{17,1},{2,18},{18,2},{3,19},{19,3},{4,20},{20... | collective-permute-start | bytes 1966088 | tf_op jit(solution)/shard_map/ppermute | solution.py:994
  42.0 10.5 %collective-permute-start.9 = (bf16[8,80,512]{2,1,0:T(8,128)(2,1)S(1)}, bf16[8,80,512]{2,1,0:T(8,128)(2,1)S(1)}, u32[]{:S(2)}, u32[]{:S(2)}) collective-permute-start(bf16[8,80,512]{2,1,0:T(8,128)(2,1)S(1)} %collective-permute-done.5.refs_3_), channel_id=1, source_target_pairs={{0,16},{16,0},{1,17},{17,1},{2,18},{18,2},{3,19},{19,3},{4,20},{20... | collective-permute-start | bytes 1966088 | tf_op jit(solution)/shard_map/ppermute | solution.py:994
  42.5 9.9 %collective-permute-start.10 = (bf16[4,144,512]{2,1,0:T(8,128)(2,1)S(1)}, bf16[4,144,512]{2,1,0:T(8,128)(2,1)S(1)}, u32[]{:S(2)}, u32[]{:S(2)}) collective-permute-start(bf16[4,144,512]{2,1,0:T(8,128)(2,1)S(1)} %constant_dynamic-update-slice_fusion.8), channel_id=1, source_target_pairs={{0,1},{1,0},{2,3},{3,2},{4,5},{5,4},{6,7},{7,6},{8,9},{9,8},{10,11... | collective-permute-start | bytes 1769480 | tf_op jit(solution)/shard_map/ppermute | solution.py:990
  44.1 6.4 %collective-permute-start.11 = (bf16[2,64,512]{2,1,0:T(8,128)(2,1)S(1)}, bf16[2,64,512]{2,1,0:T(8,128)(2,1)S(1)}, u32[]{:S(2)}, u32[]{:S(2)}) collective-permute-start(bf16[2,64,512]{2,1,0:T(8,128)(2,1)S(1)} %constant_dynamic-update-slice_fusion.10), channel_id=1, source_target_pairs={{0,4},{1,5},{2,6},{3,7},{4,0},{5,1},{6,2},{7,3},{8,12},{9,13},{10,... | collective-permute-start | bytes 393224 | tf_op jit(solution)/shard_map/ppermute | solution.py:990
  52.5 13.1 %collective-permute-start.14 = (bf16[8,144,512]{2,1,0:T(8,128)(2,1)S(1)}, bf16[8,144,512]{2,1,0:T(8,128)(2,1)S(1)}, u32[]{:S(2)}, u32[]{:S(2)}) collective-permute-start(bf16[8,144,512]{2,1,0:T(8,128)(2,1)S(1)} %constant_dynamic-update-slice_fusion.12.own_low), channel_id=1, source_target_pairs={{0,16},{16,0},{1,17},{17,1},{2,18},{18,2},{3,19},{19,3},{4,20},{20... | collective-permute-start | bytes 3538952 | tf_op jit(solution)/shard_map/ppermute | solution.py:994
  52.6 22.4 %collective-permute-start.15 = (bf16[8,144,512]{2,1,0:T(8,128)(2,1)S(1)}, bf16[8,144,512]{2,1,0:T(8,128)(2,1)S(1)}, u32[]{:S(2)}, u32[]{:S(2)}) collective-permute-start(bf16[8,144,512]{2,1,0:T(8,128)(2,1)S(1)} %constant_dynamic-update-slice_fusion.12.own_low), channel_id=1, source_target_pairs={{0,2},{1,3},{2,0},{3,1},{4,6},{5,7},{6,4},{7,5},{8,10},{9,11},{10,... | collective-permute-start | bytes 3538952 | tf_op jit(solution)/shard_map/ppermute | solution.py:990
  54.2 11.3 %collective-permute-start.13 = (bf16[1,176,512]{2,1,0:T(8,128)(2,1)S(1)}, bf16[1,176,512]{2,1,0:T(8,128)(2,1)S(1)}, u32[]{:S(2)}, u32[]{:S(2)}) collective-permute-start(bf16[1,176,512]{2,1,0:T(8,128)(2,1)S(1)} %maximum_bitcast_fusion), channel_id=1, source_target_pairs={{0,8},{1,9},{2,10},{3,11},{4,12},{5,13},{6,14},{7,15},{8,0},{9,1},... | collective-permute-start | bytes 540680 | tf_op jit(solution)/shard_map/ppermute | solution.py:990
  56.3 9.3 %collective-permute-start.12 = (bf16[4,64,512]{2,1,0:T(8,128)(2,1)S(1)}, bf16[4,64,512]{2,1,0:T(8,128)(2,1)S(1)}, u32[]{:S(2)}, u32[]{:S(2)}) collective-permute-start(bf16[4,64,512]{2,1,0:T(8,128)(2,1)S(1)} %pad_maximum_fusion.5), channel_id=1, source_target_pairs={{0,1},{1,0},{2,3},{3,2},{4,5},{5,4},{6,7},{7,6},{8,9},{9,8},{10,11... | collective-permute-start | bytes 786440 | tf_op jit(solution)/shard_map/ppermute | solution.py:990
  64.7 30.6 %copy-start.6 = (f32[16,512]{1,0:T(8,128)}, f32[16,512]{1,0:T(8,128)S(1)}, u32[]{:S(2)}) copy-start(f32[16,512]{1,0:T(8,128)S(1)} %get-tuple-element.258.vecs.refs_3_.refs_11_) | copy-start | bytes 98308
  65.7 12.0 %collective-permute-start.18 = (bf16[8,64,512]{2,1,0:T(8,128)(2,1)S(1)}, bf16[8,64,512]{2,1,0:T(8,128)(2,1)S(1)}, u32[]{:S(2)}, u32[]{:S(2)}) collective-permute-start(bf16[8,64,512]{2,1,0:T(8,128)(2,1)S(1)} %constant_dynamic-update-slice_fusion.14.refs_4_), channel_id=1, source_target_pairs={{0,16},{16,0},{1,17},{17,1},{2,18},{18,2},{3,19},{19,3},{4,20},{20... | collective-permute-start | bytes 1572872 | tf_op jit(solution)/shard_map/ppermute | solution.py:994
  65.8 11.9 %collective-permute-start.16 = (bf16[8,64,512]{2,1,0:T(8,128)(2,1)S(1)}, bf16[8,64,512]{2,1,0:T(8,128)(2,1)S(1)}, u32[]{:S(2)}, u32[]{:S(2)}) collective-permute-start(bf16[8,64,512]{2,1,0:T(8,128)(2,1)S(1)} %constant_dynamic-update-slice_fusion.14.refs_4_), channel_id=1, source_target_pairs={{0,2},{1,3},{2,0},{3,1},{4,6},{5,7},{6,4},{7,5},{8,10},{9,11},{10,... | collective-permute-start | bytes 1572872 | tf_op jit(solution)/shard_map/ppermute | solution.py:990
  67.0 10.7 %collective-permute-start.17 = (bf16[2,176,512]{2,1,0:T(8,128)(2,1)S(1)}, bf16[2,176,512]{2,1,0:T(8,128)(2,1)S(1)}, u32[]{:S(2)}, u32[]{:S(2)}) collective-permute-start(bf16[2,176,512]{2,1,0:T(8,128)(2,1)S(1)} %pad_maximum_fusion.3), channel_id=1, source_target_pairs={{0,4},{1,5},{2,6},{3,7},{4,0},{5,1},{6,2},{7,3},{8,12},{9,13},{10,... | collective-permute-start | bytes 1081352 | tf_op jit(solution)/shard_map/ppermute | solution.py:990
  77.7 3.4 %collective-permute-start.19 = (bf16[8,144,512]{2,1,0:T(8,128)(2,1)S(1)}, bf16[8,144,512]{2,1,0:T(8,128)(2,1)S(1)}, u32[]{:S(2)}, u32[]{:S(2)}) collective-permute-start(bf16[8,144,512]{2,1,0:T(8,128)(2,1)S(1)} %collective-permute-done.15.own_high), channel_id=1, source_target_pairs={{0,16},{16,0},{1,17},{17,1},{2,18},{18,2},{3,19},{19,3},{4,20},{20... | collective-permute-start | bytes 3538952 | tf_op jit(solution)/shard_map/ppermute | solution.py:994
  78.6 12.8 %collective-permute-start.21 = (bf16[8,64,512]{2,1,0:T(8,128)(2,1)S(1)}, bf16[8,64,512]{2,1,0:T(8,128)(2,1)S(1)}, u32[]{:S(2)}, u32[]{:S(2)}) collective-permute-start(bf16[8,64,512]{2,1,0:T(8,128)(2,1)S(1)} %collective-permute-done.16.refs_5_), channel_id=1, source_target_pairs={{0,16},{16,0},{1,17},{17,1},{2,18},{18,2},{3,19},{19,3},{4,20},{20... | collective-permute-start | bytes 1572872 | tf_op jit(solution)/shard_map/ppermute | solution.py:994
  78.8 12.7 %collective-permute-start.20 = (bf16[4,176,512]{2,1,0:T(8,128)(2,1)S(1)}, bf16[4,176,512]{2,1,0:T(8,128)(2,1)S(1)}, u32[]{:S(2)}, u32[]{:S(2)}) collective-permute-start(bf16[4,176,512]{2,1,0:T(8,128)(2,1)S(1)} %pad_maximum_fusion.1), channel_id=1, source_target_pairs={{0,1},{1,0},{2,3},{3,2},{4,5},{5,4},{6,7},{7,6},{8,9},{9,8},{10,11... | collective-permute-start | bytes 2162696 | tf_op jit(solution)/shard_map/ppermute | solution.py:990
  91.5 3.8 %collective-permute-start.22 = (f32[256,512]{1,0:T(8,128)S(1)}, f32[256,512]{1,0:T(8,128)S(1)}, u32[]{:S(2)}, u32[]{:S(2)}) collective-permute-start(f32[256,512]{1,0:T(8,128)S(1)} %get-tuple-element.267), channel_id=1, source_target_pairs={{0,16},{1,17},{2,18},{3,19},{4,20},{5,21},{6,22},{7,23},{8,24},{9,... | collective-permute-start | bytes 1572872 | tf_op jit(solution)/shard_map/ppermute | solution.py:1192
  93.9 22.7 %collective-permute-start.24 = (bf16[8,176,512]{2,1,0:T(8,128)(2,1)S(1)}, bf16[8,176,512]{2,1,0:T(8,128)(2,1)S(1)}, u32[]{:S(2)}, u32[]{:S(2)}) collective-permute-start(bf16[8,176,512]{2,1,0:T(8,128)(2,1)S(1)} %constant_dynamic-update-slice_fusion.17.own_low), channel_id=1, source_target_pairs={{0,16},{16,0},{1,17},{17,1},{2,18},{18,2},{3,19},{19,3},{4,20},{20... | collective-permute-start | bytes 4325384 | tf_op jit(solution)/shard_map/ppermute | solution.py:994
  94.0 22.6 %collective-permute-start.23 = (bf16[8,176,512]{2,1,0:T(8,128)(2,1)S(1)}, bf16[8,176,512]{2,1,0:T(8,128)(2,1)S(1)}, u32[]{:S(2)}, u32[]{:S(2)}) collective-permute-start(bf16[8,176,512]{2,1,0:T(8,128)(2,1)S(1)} %constant_dynamic-update-slice_fusion.17.own_low), channel_id=1, source_target_pairs={{0,2},{1,3},{2,0},{3,1},{4,6},{5,7},{6,4},{7,5},{8,10},{9,11},{10,... | collective-permute-start | bytes 4325384 | tf_op jit(solution)/shard_map/ppermute | solution.py:990
  117.7 26.7 %copy-start.9 = (s32[4]{0:T(128)S(1)}, s32[4]{0:T(128)}, u32[]{:S(2)}) copy-start(s32[4]{0:T(128)} %pad_add_fusion.scalars.refs_0_) | copy-start | bytes 52
  117.7 6.9 %collective-permute-start.25 = (bf16[8,176,512]{2,1,0:T(8,128)(2,1)S(1)}, bf16[8,176,512]{2,1,0:T(8,128)(2,1)S(1)}, u32[]{:S(2)}, u32[]{:S(2)}) collective-permute-start(bf16[8,176,512]{2,1,0:T(8,128)(2,1)S(1)} %collective-permute-done.23.own_high), channel_id=1, source_target_pairs={{0,16},{16,0},{1,17},{17,1},{2,18},{18,2},{3,19},{19,3},{4,20},{20... | collective-permute-start | bytes 4325384 | tf_op jit(solution)/shard_map/ppermute | solution.py:994
  144.0 8.2 %collective-permute-start.26 = (bf16[16,176,512]{2,1,0:T(8,128)(2,1)}, bf16[16,176,512]{2,1,0:T(8,128)(2,1)S(1)}, u32[]{:S(2)}, u32[]{:S(2)}) collective-permute-start(bf16[16,176,512]{2,1,0:T(8,128)(2,1)} %get-tuple-element.295), channel_id=1, source_target_pairs={{0,16},{16,0},{1,17},{17,1},{2,18},{18,2},{3,19},{19,3},{4,20},{20... | collective-permute-start | bytes 8650760 | tf_op jit(solution)/shard_map/ppermute | solution.py:994
  152.2 57.4 %copy-start.45 = (bf16[16,176,512]{2,1,0:T(8,128)(2,1)}, bf16[16,176,512]{2,1,0:T(8,128)(2,1)S(1)}, u32[]{:S(2)}) copy-start(bf16[16,176,512]{2,1,0:T(8,128)(2,1)S(1)} %collective-permute-done.26.refs_17_) | copy-start | bytes 8650756
  154.1 19.3 %collective-permute-start.27 = (bf16[8,176,512]{2,1,0:T(8,128)(2,1)}, bf16[8,176,512]{2,1,0:T(8,128)(2,1)}, u32[]{:S(2)}, u32[]{:S(2)}) collective-permute-start(bf16[8,176,512]{2,1,0:T(8,128)(2,1)} %add_convert_fusion), channel_id=1, source_target_pairs={{0,2},{1,3},{2,0},{3,1},{4,6},{5,7},{6,4},{7,5},{8,10},{9,11},{10,... | collective-permute-start | bytes 4325384 | tf_op jit(solution)/shard_map/ppermute | solution.py:990
  164.4 61.0 %copy-start.2 = (bf16[16,64,512]{2,1,0:T(8,128)(2,1)}, bf16[16,64,512]{2,1,0:T(8,128)(2,1)S(1)}, u32[]{:S(2)}) copy-start(bf16[16,64,512]{2,1,0:T(8,128)(2,1)S(1)} %get-tuple-element.316.refs_10_) | copy-start | bytes 3145732
  164.4 9.1 %collective-permute-start.28 = (bf16[16,64,512]{2,1,0:T(8,128)(2,1)S(1)}, bf16[16,64,512]{2,1,0:T(8,128)(2,1)}, u32[]{:S(2)}, u32[]{:S(2)}) collective-permute-start(bf16[16,64,512]{2,1,0:T(8,128)(2,1)S(1)} %get-tuple-element.309), channel_id=1, source_target_pairs={{0,16},{16,0},{1,17},{17,1},{2,18},{18,2},{3,19},{19,3},{4,20},{20... | collective-permute-start | bytes 3145736 | tf_op jit(solution)/shard_map/ppermute | solution.py:994
  174.7 14.5 %collective-permute-start.30 = (bf16[8,64,512]{2,1,0:T(8,128)(2,1)S(1)}, bf16[8,64,512]{2,1,0:T(8,128)(2,1)S(1)}, u32[]{:S(2)}, u32[]{:S(2)}) collective-permute-start(bf16[8,64,512]{2,1,0:T(8,128)(2,1)S(1)} %add_convert_fusion.5), channel_id=1, source_target_pairs={{0,2},{1,3},{2,0},{3,1},{4,6},{5,7},{6,4},{7,5},{8,10},{9,11},{10,... | collective-permute-start | bytes 1572872 | tf_op jit(solution)/shard_map/ppermute | solution.py:990
  176.6 14.9 %collective-permute-start.29 = (bf16[4,176,512]{2,1,0:T(8,128)(2,1)S(1)}, bf16[4,176,512]{2,1,0:T(8,128)(2,1)S(1)}, u32[]{:S(2)}, u32[]{:S(2)}) collective-permute-start(bf16[4,176,512]{2,1,0:T(8,128)(2,1)S(1)} %add_convert_fusion.2), channel_id=1, source_target_pairs={{0,1},{1,0},{2,3},{3,2},{4,5},{5,4},{6,7},{7,6},{8,9},{9,8},{10,11... | collective-permute-start | bytes 2162696 | tf_op jit(solution)/shard_map/ppermute | solution.py:990
  191.5 14.3 %collective-permute-start.33 = (bf16[16,144,512]{2,1,0:T(8,128)(2,1)}, bf16[16,144,512]{2,1,0:T(8,128)(2,1)S(1)}, u32[]{:S(2)}, u32[]{:S(2)}) collective-permute-start(bf16[16,144,512]{2,1,0:T(8,128)(2,1)} %get-tuple-element.329), channel_id=1, source_target_pairs={{0,16},{16,0},{1,17},{17,1},{2,18},{18,2},{3,19},{19,3},{4,20},{20... | collective-permute-start | bytes 7077896 | tf_op jit(solution)/shard_map/ppermute | solution.py:994
  192.8 10.2 %collective-permute-start.32 = (bf16[4,64,512]{2,1,0:T(8,128)(2,1)S(1)}, bf16[4,64,512]{2,1,0:T(8,128)(2,1)S(1)}, u32[]{:S(2)}, u32[]{:S(2)}) collective-permute-start(bf16[4,64,512]{2,1,0:T(8,128)(2,1)S(1)} %add_convert_fusion.9), channel_id=1, source_target_pairs={{0,1},{1,0},{2,3},{3,2},{4,5},{5,4},{6,7},{7,6},{8,9},{9,8},{10,11... | collective-permute-start | bytes 786440 | tf_op jit(solution)/shard_map/ppermute | solution.py:990
  195.5 10.4 %collective-permute-start.31 = (bf16[2,176,512]{2,1,0:T(8,128)(2,1)S(1)}, bf16[2,176,512]{2,1,0:T(8,128)(2,1)S(1)}, u32[]{:S(2)}, u32[]{:S(2)}) collective-permute-start(bf16[2,176,512]{2,1,0:T(8,128)(2,1)S(1)} %add_convert_fusion.6), channel_id=1, source_target_pairs={{0,4},{1,5},{2,6},{3,7},{4,0},{5,1},{6,2},{7,3},{8,12},{9,13},{10,... | collective-permute-start | bytes 1081352 | tf_op jit(solution)/shard_map/ppermute | solution.py:990
  206.9 15.1 %collective-permute-start.35 = (bf16[2,64,512]{2,1,0:T(8,128)(2,1)S(1)}, bf16[2,64,512]{2,1,0:T(8,128)(2,1)S(1)}, u32[]{:S(2)}, u32[]{:S(2)}) collective-permute-start(bf16[2,64,512]{2,1,0:T(8,128)(2,1)S(1)} %add_convert_fusion.14), channel_id=1, source_target_pairs={{0,4},{1,5},{2,6},{3,7},{4,0},{5,1},{6,2},{7,3},{8,12},{9,13},{10,... | collective-permute-start | bytes 393224 | tf_op jit(solution)/shard_map/ppermute | solution.py:990
  209.1 16.3 %collective-permute-start.36 = (bf16[8,144,512]{2,1,0:T(8,128)(2,1)S(1)}, bf16[8,144,512]{2,1,0:T(8,128)(2,1)S(1)}, u32[]{:S(2)}, u32[]{:S(2)}) collective-permute-start(bf16[8,144,512]{2,1,0:T(8,128)(2,1)S(1)} %add_convert_fusion.1), channel_id=1, source_target_pairs={{0,2},{1,3},{2,0},{3,1},{4,6},{5,7},{6,4},{7,5},{8,10},{9,11},{10,... | collective-permute-start | bytes 3538952 | tf_op jit(solution)/shard_map/ppermute | solution.py:990
  210.7 11.4 %collective-permute-start.34 = (bf16[1,176,512]{2,1,0:T(8,128)(2,1)S(1)}, bf16[1,176,512]{2,1,0:T(8,128)(2,1)S(1)}, u32[]{:S(2)}, u32[]{:S(2)}) collective-permute-start(bf16[1,176,512]{2,1,0:T(8,128)(2,1)S(1)} %add_convert_fusion.10), channel_id=1, source_target_pairs={{0,8},{1,9},{2,10},{3,11},{4,12},{5,13},{6,14},{7,15},{8,0},{9,1},... | collective-permute-start | bytes 540680 | tf_op jit(solution)/shard_map/ppermute | solution.py:990
  222.0 39.6 %copy-start.3 = (bf16[16,64,512]{2,1,0:T(8,128)(2,1)}, bf16[16,64,512]{2,1,0:T(8,128)(2,1)S(1)}, u32[]{:S(2)}) copy-start(bf16[16,64,512]{2,1,0:T(8,128)(2,1)S(1)} %get-tuple-element.341.refs_2_) | copy-start | bytes 3145732
  225.4 30.5 %copy-start.48 = (bf16[8,144,512]{2,1,0:T(8,128)(2,1)}, bf16[8,144,512]{2,1,0:T(8,128)(2,1)S(1)}, u32[]{:S(2)}) copy-start(bf16[8,144,512]{2,1,0:T(8,128)(2,1)S(1)} %collective-permute-done.36.refs_6_) | copy-start | bytes 3538948
  225.4 9.0 %collective-permute-start.38 = (bf16[16,64,512]{2,1,0:T(8,128)(2,1)S(1)}, bf16[16,64,512]{2,1,0:T(8,128)(2,1)S(1)}, u32[]{:S(2)}, u32[]{:S(2)}) collective-permute-start(bf16[16,64,512]{2,1,0:T(8,128)(2,1)S(1)} %get-tuple-element.358), channel_id=1, source_target_pairs={{0,16},{16,0},{1,17},{17,1},{2,18},{18,2},{3,19},{19,3},{4,20},{20... | collective-permute-start | bytes 3145736 | tf_op jit(solution)/shard_map/ppermute | solution.py:994
  226.5 7.8 %collective-permute-start.37 = (bf16[1,64,512]{2,1,0:T(8,128)(2,1)S(1)}, bf16[1,64,512]{2,1,0:T(8,128)(2,1)S(1)}, u32[]{:S(2)}, u32[]{:S(2)}) collective-permute-start(bf16[1,64,512]{2,1,0:T(8,128)(2,1)S(1)} %add_convert_fusion.17), channel_id=1, source_target_pairs={{0,8},{1,9},{2,10},{3,11},{4,12},{5,13},{6,14},{7,15},{8,0},{9,1},... | collective-permute-start | bytes 196616 | tf_op jit(solution)/shard_map/ppermute | solution.py:990
  228.5 9.9 %collective-permute-start.39 = (bf16[4,144,512]{2,1,0:T(8,128)(2,1)S(1)}, bf16[4,144,512]{2,1,0:T(8,128)(2,1)S(1)}, u32[]{:S(2)}, u32[]{:S(2)}) collective-permute-start(bf16[4,144,512]{2,1,0:T(8,128)(2,1)S(1)} %add_convert_fusion.3), channel_id=1, source_target_pairs={{0,1},{1,0},{2,3},{3,2},{4,5},{5,4},{6,7},{7,6},{8,9},{9,8},{10,11... | collective-permute-start | bytes 1769480 | tf_op jit(solution)/shard_map/ppermute | solution.py:990
  234.3 27.3 %copy-start.5 = (bf16[16,16,512]{2,1,0:T(8,128)(2,1)}, bf16[16,16,512]{2,1,0:T(8,128)(2,1)S(1)}, u32[]{:S(2)}) copy-start(bf16[16,16,512]{2,1,0:T(8,128)(2,1)S(1)} %get-tuple-element.361.refs_22_) | copy-start | bytes 786436
  234.3 27.3 %copy-start.49 = (bf16[16,64,512]{2,1,0:T(8,128)(2,1)}, bf16[16,64,512]{2,1,0:T(8,128)(2,1)S(1)}, u32[]{:S(2)}) copy-start(bf16[16,64,512]{2,1,0:T(8,128)(2,1)S(1)} %collective-permute-done.38.refs_3_) | copy-start | bytes 3145732
  234.3 1.6 collective-permute-start.40
  235.9 25.7 %copy-start.55 = (bf16[16,16,512]{2,1,0:T(8,128)(2,1)}, bf16[16,16,512]{2,1,0:T(8,128)(2,1)S(1)}, u32[]{:S(2)}) copy-start(bf16[16,16,512]{2,1,0:T(8,128)(2,1)S(1)} %collective-permute-done.40.refs_23_) | copy-start | bytes 786436
  236.0 12.0 %collective-permute-start.41 = (bf16[8,80,512]{2,1,0:T(8,128)(2,1)S(1)}, bf16[8,80,512]{2,1,0:T(8,128)(2,1)S(1)}, u32[]{:S(2)}, u32[]{:S(2)}) collective-permute-start(bf16[8,80,512]{2,1,0:T(8,128)(2,1)S(1)} %pad_maximum_fusion.2), channel_id=1, source_target_pairs={{0,2},{1,3},{2,0},{3,1},{4,6},{5,7},{6,4},{7,5},{8,10},{9,11},{10,... | collective-permute-start | bytes 1966088 | tf_op jit(solution)/shard_map/ppermute | solution.py:990
  239.9 8.2 %collective-permute-start.42 = (bf16[2,144,512]{2,1,0:T(8,128)(2,1)S(1)}, bf16[2,144,512]{2,1,0:T(8,128)(2,1)S(1)}, u32[]{:S(2)}, u32[]{:S(2)}) collective-permute-start(bf16[2,144,512]{2,1,0:T(8,128)(2,1)S(1)} %add_convert_fusion.7), channel_id=1, source_target_pairs={{0,4},{1,5},{2,6},{3,7},{4,0},{5,1},{6,2},{7,3},{8,12},{9,13},{10,... | collective-permute-start | bytes 884744 | tf_op jit(solution)/shard_map/ppermute | solution.py:990
  248.2 7.1 %collective-permute-start.44 = (bf16[4,80,512]{2,1,0:T(8,128)(2,1)S(1)}, bf16[4,80,512]{2,1,0:T(8,128)(2,1)S(1)}, u32[]{:S(2)}, u32[]{:S(2)}) collective-permute-start(bf16[4,80,512]{2,1,0:T(8,128)(2,1)S(1)} %pad_maximum_fusion.4), channel_id=1, source_target_pairs={{0,1},{1,0},{2,3},{3,2},{4,5},{5,4},{6,7},{7,6},{8,9},{9,8},{10,11... | collective-permute-start | bytes 983048 | tf_op jit(solution)/shard_map/ppermute | solution.py:990
  255.5 6.1 %collective-permute-start.45 = (bf16[2,80,512]{2,1,0:T(8,128)(2,1)S(1)}, bf16[2,80,512]{2,1,0:T(8,128)(2,1)S(1)}, u32[]{:S(2)}, u32[]{:S(2)}) collective-permute-start(bf16[2,80,512]{2,1,0:T(8,128)(2,1)S(1)} %pad_maximum_fusion.6), channel_id=1, source_target_pairs={{0,4},{1,5},{2,6},{3,7},{4,0},{5,1},{6,2},{7,3},{8,12},{9,13},{10,... | collective-permute-start | bytes 491528 | tf_op jit(solution)/shard_map/ppermute | solution.py:990
  256.9 9.8 %collective-permute-start.43 = (bf16[1,144,512]{2,1,0:T(8,128)(2,1)S(1)}, bf16[1,144,512]{2,1,0:T(8,128)(2,1)S(1)}, u32[]{:S(2)}, u32[]{:S(2)}) collective-permute-start(bf16[1,144,512]{2,1,0:T(8,128)(2,1)S(1)} %add_convert_fusion.11), channel_id=1, source_target_pairs={{0,8},{1,9},{2,10},{3,11},{4,12},{5,13},{6,14},{7,15},{8,0},{9,1},... | collective-permute-start | bytes 442376 | tf_op jit(solution)/shard_map/ppermute | solution.py:990
  261.7 5.9 %collective-permute-start.46 = (bf16[1,80,512]{2,1,0:T(8,128)(2,1)S(1)}, bf16[1,80,512]{2,1,0:T(8,128)(2,1)S(1)}, u32[]{:S(2)}, u32[]{:S(2)}) collective-permute-start(bf16[1,80,512]{2,1,0:T(8,128)(2,1)S(1)} %pad_maximum_fusion.7), channel_id=1, source_target_pairs={{0,8},{1,9},{2,10},{3,11},{4,12},{5,13},{6,14},{7,15},{8,0},{9,1},... | collective-permute-start | bytes 245768 | tf_op jit(solution)/shard_map/ppermute | solution.py:990
  273.1 15.3 %collective-permute-start.54 = (f32[256,512]{1,0:T(8,128)}, f32[256,512]{1,0:T(8,128)S(1)}, u32[]{:S(2)}, u32[]{:S(2)}) collective-permute-start(f32[256,512]{1,0:T(8,128)} %get-tuple-element.369), channel_id=1, source_target_pairs={{0,16},{16,0},{1,17},{17,1},{2,18},{18,2},{3,19},{19,3},{4,20},{20... | collective-permute-start | bytes 1572872 | tf_op jit(solution)/shard_map/ppermute | solution.py:994
  273.1 2.1 collective-permute-start.47
  276.0 5.4 %collective-permute-start.50 = (f32[8,128]{1,0:T(8,128)S(1)}, f32[8,128]{1,0:T(8,128)S(1)}, u32[]{:S(2)}, u32[]{:S(2)}) collective-permute-start(f32[8,128]{1,0:T(8,128)S(1)} %add.235), channel_id=1, source_target_pairs={{0,12},{1,13},{2,14},{3,15},{4,8},{5,9},{6,10},{7,11},{8,4},{9,5},... | collective-permute-start | bytes 12296 | tf_op jit(solution)/shard_map/ppermute | solution.py:990
  277.5 3.9 %collective-permute-start.49 = (f32[8,128]{1,0:T(8,128)S(1)}, f32[8,128]{1,0:T(8,128)S(1)}, u32[]{:S(2)}, u32[]{:S(2)}) collective-permute-start(f32[8,128]{1,0:T(8,128)S(1)} %add.235), channel_id=1, source_target_pairs={{0,4},{1,5},{2,6},{3,7},{4,0},{5,1},{6,2},{7,3},{8,12},{9,13},{10,... | collective-permute-start | bytes 12296 | tf_op jit(solution)/shard_map/ppermute | solution.py:990
  278.0 4.5 %collective-permute-start.48 = (f32[8,128]{1,0:T(8,128)S(1)}, f32[8,128]{1,0:T(8,128)S(1)}, u32[]{:S(2)}, u32[]{:S(2)}) collective-permute-start(f32[8,128]{1,0:T(8,128)S(1)} %add.235), channel_id=1, source_target_pairs={{0,8},{1,9},{2,10},{3,11},{4,12},{5,13},{6,14},{7,15},{8,0},{9,1},... | collective-permute-start | bytes 12296 | tf_op jit(solution)/shard_map/ppermute | solution.py:990
  282.6 4.5 %collective-permute-start.53 = (f32[8,128]{1,0:T(8,128)S(1)}, f32[8,128]{1,0:T(8,128)S(1)}, u32[]{:S(2)}, u32[]{:S(2)}) collective-permute-start(f32[8,128]{1,0:T(8,128)S(1)} %add_add_fusion.1), channel_id=1, source_target_pairs={{0,3},{1,2},{2,1},{3,0},{4,7},{5,6},{6,5},{7,4},{8,11},{9,10},{10,... | collective-permute-start | bytes 12296 | tf_op jit(solution)/shard_map/ppermute | solution.py:990
  284.3 3.6 %collective-permute-start.52 = (f32[8,128]{1,0:T(8,128)S(1)}, f32[8,128]{1,0:T(8,128)S(1)}, u32[]{:S(2)}, u32[]{:S(2)}) collective-permute-start(f32[8,128]{1,0:T(8,128)S(1)} %add_add_fusion.1), channel_id=1, source_target_pairs={{0,2},{1,3},{2,0},{3,1},{4,6},{5,7},{6,4},{7,5},{8,10},{9,11},{10,... | collective-permute-start | bytes 12296 | tf_op jit(solution)/shard_map/ppermute | solution.py:990
  284.8 3.6 %collective-permute-start.51 = (f32[8,128]{1,0:T(8,128)S(1)}, f32[8,128]{1,0:T(8,128)S(1)}, u32[]{:S(2)}, u32[]{:S(2)}) collective-permute-start(f32[8,128]{1,0:T(8,128)S(1)} %add_add_fusion.1), channel_id=1, source_target_pairs={{0,1},{1,0},{2,3},{3,2},{4,5},{5,4},{6,7},{7,6},{8,9},{9,8},{10,11... | collective-permute-start | bytes 12296 | tf_op jit(solution)/shard_map/ppermute | solution.py:990
  (67 other events, 876.2 us)
where the time goes:
time: 298 us; the launch traced here: 293 us
  Pallas kernels  123 us (41%)
  waiting for transfers between devices  70.7 us (24%)
  starting transfers between devices  66.6 us (22%)
  other arithmetic  19.4 us (7%)
  local copies, waits for them, and re-layouts  9.45 us (3%)
    ppermute x38, waiting for transfers between devices, spread(): return lax.ppermute(value, ('section', 'dp'), pairs)  63 us
    ppermute x38, starting transfers between devices, spread(): return lax.ppermute(value, ('section', 'dp'), pairs)  52.4 us
    pallas_call x2, Pallas kernels, run_attend(): call(attend, 'attend', [SMEM] + [VMEM] * 5, (half_shape(SEG, D), half_sha...  20.3 us
    pallas_call x2, Pallas kernels, run_attend_back_rest(): call(functools.partial(attend_back, bits, True), 'attend_back_rest', [SME...  19.3 us
    pallas_call x1, Pallas kernels, run_top(): call(functools.partial(top_kernel, bits, streams), 'top_kernel', [SMEM, V...  18.2 us
    convert_element_type x20, other arithmetic, shrink(): sent.append(total.astype(BF16))  13.6 us
    pallas_call x2, Pallas kernels, run_attend_back(): call(functools.partial(attend_back, bits, False), 'attend_back', [SMEM, V...  13.4 us
    ppermute x16, starting transfers between devices, swap(): return lax.ppermute(value, 'section', [(0, 1), (1, 0)])  12 us
  transfers between devices with their start and end apart: 55, of which 32 were waited for; matrix products, arithmetic and copies ran while one was open for 5% of the time, Pallas kernels for 33%

commit v1 on v0

--- a/solution.py
+++ b/solution.py
@@ -867,7 +867,7 @@
         [VMEM] * 2,
         [held(4, D, D), DMA((3,))],
         5,
-        50,
+        40,
     )(scalars, saved, *grads, grad_mixed, vecs, memory, hidden)
 
 
@@ -880,7 +880,7 @@
         [ANY] * 2,
         [wide(ROWS, D), wide(BLOCK, D), held(D, D), DMA, held(D, BLOCK), DMA, held(4, D, D), DMA((3,))],
         5,
-        50,
+        40,
     )(scalars, saved, *grads, grad_mixed, vecs, frames, *small_grads)
 
 
@@ -930,7 +930,7 @@
         + BACK_HELD
         + [DMA, DMA((3,)), DMA((3,))],
         21,
-        56,
+        55,
     )(scalars, residual, attended, targets, vecs, *pieces)
 
 
@@ -945,7 +945,7 @@
         [VMEM] * 3,
         [pltpu.VMEM(item.shape[1:], item.dtype) for item in flat] + [DMA((len(flat),))],
         3,
-        56,
+        40,
     )(scalars, loss, *flat)
 
 
@@ -1273,11 +1273,18 @@
         got = shrink([sum_d, sum_e], pair, sum_de)
         if pair == last:
             sum_c.append(got_c)
-            got, got_c = fence(got, shrink([sum_c], near))
+            got, got_c, one_a, one_b = fence(got, shrink([sum_c], near), part(sum_a, 0, 1), part(sum_b, 0, 1))
             sum_c.append(got_c)
-            sum_c.append(shrink([sum_c], far))
+            got_c = shrink([sum_c], far)
+        if pair == near:
+            one_d = part(sum_d + [item[:, :64] for item in sum_de], 0, 1)
+            one_e = part(sum_e + [item[:, 64:] for item in sum_de], 0, 1)
+            got, one_c, one_d, one_e = fence(got, part(sum_c, 0, 1), one_d, one_e)
+            one_d, one_e = one_d + got[:1, :64].astype(F32), one_e + got[:1, 64:].astype(F32)
         sum_de.append(got)
-    kept, sent, total = run_finish(scalars, loss, sum_d, sum_c, sum_b, sum_a, sum_e, sum_de)
+    kept, sent, total = run_finish(
+        scalars, loss, [one_d], [one_c, got_c], [one_b], [one_a], [one_e], sum_de[3:]
+    )
     got = swap(sent)
     return tuple(run_update(scalars, add_up(total, bits), kept, got, state))
 

time: 298 us -> 287 us (0.963)
  other arithmetic: 19.4 us -> 12.8 us
  Pallas kernels: 123 us -> 120 us
    convert_element_type x20, other arithmetic: 13.6 us -> 5.6 us  [shrink(): sent.append(total.astype(BF16))]
    unnamed x165 -> x137, local copies, waits for them, and re-layouts: 8.53 us -> 6.93 us
  transfers between devices with their start and end apart: 55 -> 55, of which waited for: 32 -> 32; matrix products, arithmetic and copies ran while one was open for 5% -> 4% of each run, Pallas kernels for 33% -> 34%
where the time goes in v1:
time: 287 us; the launch traced here: 282 us
  Pallas kernels  120 us (42%)
  waiting for transfers between devices  72.1 us (25%)
  starting transfers between devices  66.3 us (23%)
  other arithmetic  12.8 us (4%)
  local copies, waits for them, and re-layouts  7.86 us (3%)
  between operations  2.89 us (1%)
    ppermute x38, waiting for transfers between devices, spread(): return lax.ppermute(value, ('section', 'dp'), pairs)  64.7 us
    ppermute x38, starting transfers between devices, spread(): return lax.ppermute(value, ('section', 'dp'), pairs)  51.8 us
    pallas_call x2, Pallas kernels, run_attend(): call(attend, 'attend', [SMEM] + [VMEM] * 5, (half_shape(SEG, D), half_sha...  20.4 us
    pallas_call x2, Pallas kernels, run_attend_back_rest(): call(functools.partial(attend_back, bits, True), 'attend_back_rest', [SME...  19.4 us
    pallas_call x1, Pallas kernels, run_top(): call(functools.partial(top_kernel, bits, streams), 'top_kernel', [SMEM, V...  18.2 us
    pallas_call x2, Pallas kernels, run_attend_back(): call(functools.partial(attend_back, bits, False), 'attend_back', [SMEM, V...  13.5 us
    ppermute x16, starting transfers between devices, swap(): return lax.ppermute(value, 'section', [(0, 1), (1, 0)])  12.2 us
    pallas_call x1, Pallas kernels, run_feed_backward(): call(functools.partial(feed_backward, bits, base), 'feed_backward', [SMEM...  11.1 us
  transfers between devices with their start and end apart: 55, of which 32 were waited for; matrix products, arithmetic and copies ran while one was open for 4% of the time, Pallas kernels for 34%

profile of v1, /device:TPU:0, one launch (start us, length us, event | category | flops | bytes accessed | tf_op | source)
XLA Modules:
  0.0 282.1 jit_solution(10047217016072407665)
XLA Ops:
  1.9 2.2 pack_shards.1
  6.9 4.0 %collective-permute-start.1 = (bf16[1,80,512]{2,1,0:T(8,128)(2,1)S(1)}, bf16[1,80,512]{2,1,0:T(8,128)(2,1)S(1)}, u32[]{:S(2)}, u32[]{:S(2)}) collective-permute-start(bf16[1,80,512]{2,1,0:T(8,128)(2,1)S(1)} %select_bitcast_fusion), channel_id=1, source_target_pairs={{0,8},{1,9},{2,10},{3,11},{4,12},{5,13},{6,14},{7,15},{8,0},{9,1},... | collective-permute-start | bytes 245768 | tf_op jit(solution)/shard_map/ppermute | solution.py:990
  11.0 4.4 %collective-permute-done.1 = bf16[1,80,512]{2,1,0:T(8,128)(2,1)S(1)} collective-permute-done((bf16[1,80,512]{2,1,0:T(8,128)(2,1)S(1)}, bf16[1,80,512]{2,1,0:T(8,128)(2,1)S(1)}, u32[]{:S(2)}, u32[]{:S(2)}) %collective-permute-start.1) | collective-permute-done | bytes 81952 | tf_op jit(solution)/shard_map/ppermute | solution.py:990
  16.2 5.0 %collective-permute-done.2 = bf16[2,80,512]{2,1,0:T(8,128)(2,1)S(1)} collective-permute-done((bf16[2,80,512]{2,1,0:T(8,128)(2,1)S(1)}, bf16[2,80,512]{2,1,0:T(8,128)(2,1)S(1)}, u32[]{:S(2)}, u32[]{:S(2)}) %collective-permute-start.2) | collective-permute-done | bytes 163872 | tf_op jit(solution)/shard_map/ppermute | solution.py:990
  21.2 2.8 collective-permute-start.4
  24.0 1.6 collective-permute-start.3
  25.6 3.2 %fusion = (bf16[768,256]{1,0:T(8,128)(2,1)S(1)}, bf16[768,256]{1,0:T(8,128)(2,1)S(1)}) fusion(f32[256]{0:T(256)S(1)} %multiply_exponential_fusion, f32[768]{0:T(1024)S(1)} %reduce), kind=kLoop, calls=%fused_computation.8 | loop fusion | flops 589824 | bytes 790528 | tf_op jit(solution)/shard_map/convert
  28.8 1.8 collective-permute-done.4
  31.2 1.6 collective-permute-start.5
  32.8 1.8 collective-permute-start.6
  34.6 1.8 collective-permute-start.7
  36.5 4.1 %collective-permute-done.7 = bf16[1,64,512]{2,1,0:T(8,128)(2,1)S(1)} collective-permute-done((bf16[1,64,512]{2,1,0:T(8,128)(2,1)S(1)}, bf16[1,64,512]{2,1,0:T(8,128)(2,1)S(1)}, u32[]{:S(2)}, u32[]{:S(2)}) %collective-permute-start.7) | collective-permute-done | bytes 65568 | tf_op jit(solution)/shard_map/ppermute | solution.py:990
  42.5 1.6 collective-permute-start.10
  44.1 2.0 collective-permute-start.11
  46.1 4.4 %collective-permute-done.11 = bf16[2,64,512]{2,1,0:T(8,128)(2,1)S(1)} collective-permute-done((bf16[2,64,512]{2,1,0:T(8,128)(2,1)S(1)}, bf16[2,64,512]{2,1,0:T(8,128)(2,1)S(1)}, u32[]{:S(2)}, u32[]{:S(2)}) %collective-permute-start.11) | collective-permute-done | bytes 131104 | tf_op jit(solution)/shard_map/ppermute | solution.py:990
  50.5 2.0 collective-permute-done.10
  52.6 1.6 collective-permute-start.15
  54.2 2.1 collective-permute-start.13
  57.0 6.7 %project_first.1 = (bf16[512,512]{1,0:T(8,128)(2,1)S(1)}, bf16[512,512]{1,0:T(8,128)(2,1)S(1)}, bf16[768,512]{1,0:T(8,128)(2,1)S(1)}, bf16[768,512]{1,0:T(8,128)...) custom-call(s32[4]{0:T(128)S(1)} %copy-done.7, ...), custom_call_target="tpu_custom_call" | custom-call | flops 6899999744 | bytes 1048576 | tf_op jit(solution)/shard_map/project_first/pallas_call | solution.py:784
  63.7 1.8 collective-permute-done.13
  65.8 1.2 collective-permute-start.16
  67.0 1.9 collective-permute-start.17
  68.9 6.2 %attend.2 = (bf16[512,512]{1,0:T(8,128)(2,1)S(1)}, bf16[14,256,2304]{2,1,0:T(8,128)(2,1)}) custom-call(s32[4]{0:T(128)S(1)} %copy-done.7, bf16[512,512]{1,0:T(8,128)(2,1)S(1)} %get-tuple-element.255.query_u, bf16[512,512]{1,0:T(8,128)(2,1)S(1)} %get-tuple-element.256.query_v, bf16[768,512]{1,0:T(8,128)(2,1)S(1)} %get-tuple-element.257.keys, ...), custom_call_target="tpu_custom_call" | custom-call | flops 12650000384 | bytes 1048576 | tf_op jit(solution)/shard_map/attend/pallas_call | solution.py:812
  75.1 2.6 collective-permute-done.17
  78.8 1.6 collective-permute-start.20
  82.2 9.3 %feed_forward.1 = (f32[512,512]{1,0:T(8,128)S(1)}, f32[256,512]{1,0:T(8,128)S(1)}, f32[512,512]{1,0:T(8,128)S(1)}, bf16[16384,512]{1,0:T(8,128)(2,1)}) custom-call(s32[4]{0:T(128)S(1)} %copy-done.7, f32[512,512]{1,0:T(8,128)} %copy-done.39, bf16[512,512]{1,0:T(8,128)(2,1)S(1)} %get-tuple-element.263.attended, ...), custom_call_target="tpu_custom_call" | custom-call | flops 10350000128 | bytes 1048576 | tf_op jit(solution)/shard_map/feed_forward/pallas_call | solution.py:892
  91.5 2.3 collective-permute-start.22
  95.3 6.2 %project.1 = (bf16[512,512]{1,0:T(8,128)(2,1)S(1)}, bf16[512,512]{1,0:T(8,128)(2,1)S(1)}, bf16[768,512]{1,0:T(8,128)(2,1)S(1)}, bf16[768,512]{1,0:T(8,128)(2,1)S...) custom-call(s32[4]{0:T(128)S(1)} %copy-done.7, f32[256,512]{1,0:T(8,128)S(1)} %collective-permute-done.22.refs_1_.refs_12_, ...), custom_call_target="tpu_custom_call" | custom-call | flops 6899999744 | bytes 1048576 | tf_op jit(solution)/shard_map/project/pallas_call | solution.py:798
  101.6 14.2 %attend.3 = (bf16[512,512]{1,0:T(8,128)(2,1)S(1)}, bf16[14,256,2304]{2,1,0:T(8,128)(2,1)}) custom-call(s32[4]{0:T(128)S(1)} %copy-done.7, bf16[512,512]{1,0:T(8,128)(2,1)S(1)} %get-tuple-element.278.query_u, bf16[512,512]{1,0:T(8,128)(2,1)S(1)} %get-tuple-element.279.query_v, bf16[768,512]{1,0:T(8,128)(2,1)S(1)} %get-tuple-element.280.keys, ...), custom_call_target="tpu_custom_call" | custom-call | flops 12650000384 | bytes 1048576 | tf_op jit(solution)/shard_map/attend/pallas_call | solution.py:812
  118.9 4.1 %collective-permute-start.25 = (bf16[8,176,512]{2,1,0:T(8,128)(2,1)S(1)}, bf16[8,176,512]{2,1,0:T(8,128)(2,1)S(1)}, u32[]{:S(2)}, u32[]{:S(2)}) collective-permute-start(bf16[8,176,512]{2,1,0:T(8,128)(2,1)S(1)} %collective-permute-done.23.own_high), channel_id=1, source_target_pairs={{0,16},{16,0},{1,17},{17,1},{2,18},{18,2},{3,19},{19,3},{4,20},{20... | collective-permute-start | bytes 4325384 | tf_op jit(solution)/shard_map/ppermute | solution.py:994
  123.0 2.8 %collective-permute-done.25.other_high = bf16[8,176,512]{2,1,0:T(8,128)(2,1)S(1)} collective-permute-done((bf16[8,176,512]{2,1,0:T(8,128)(2,1)S(1)}, bf16[8,176,512]{2,1,0:T(8,128)(2,1)S(1)}, u32[]{:S(2)}, u32[]{:S(2)}) %collective-permute-start.25) | collective-permute-done | bytes 1441824 | tf_op jit(solution)/shard_map/ppermute | solution.py:994
  125.8 1.2 copy-done.58
  127.0 18.2 %top_kernel.1 = (bf16[16,176,512]{2,1,0:T(8,128)(2,1)}, bf16[16,176,512]{2,1,0:T(8,128)(2,1)}, f32[512,512]{1,0:T(8,128)}, bf16[512,512]{1,0:T(8,128)(2,1)}, f32...) custom-call(s32[4]{0:T(128)} %pad_add_fusion.scalars.refs_0_, f32[512,512]{1,0:T(8,128)} %copy-done.2, ...), custom_call_target="tpu_custom_call" | custom-call | flops 24149999616 | bytes 1048576 | tf_op jit(solution)/shard_map/top_kernel/pallas_call | solution.py:919
  146.7 6.8 %attend_back.2 = (bf16[512,256]{1,0:T(8,128)(2,1)S(1)}, bf16[768,256]{1,0:T(8,128)(2,1)S(1)}, bf16[768,256]{1,0:T(8,128)(2,1)S(1)}, bf16[4,512,256]{2,1,0:T(8,128)(2,1)S(1)}, f32[8,256]{1,0:T(8,128)S(1)}) custom-call(s32[4]{0:T(128)S(1)} %copy-done.8, bf16[512,512]{1,0:T(8,128)(2,1)S(1)} %copy-done.36, ...), custom_call_target="tpu_custom_call" | custom-call | flops 10350000128 | bytes 1048576 | tf_op jit(solution)/shard_map/attend_back/pallas_call | solution.py:834
  154.5 9.8 %attend_back_rest.2 = (bf16[512,256]{1,0:T(8,128)(2,1)S(1)}, bf16[768,256]{1,0:T(8,128)(2,1)S(1)}, bf16[768,256]{1,0:T(8,128)(2,1)S(1)}, f32[8,256]{1,0:T(8,128)...) custom-call(s32[4]{0:T(128)S(1)} %copy-done.8, bf16[512,512]{1,0:T(8,128)(2,1)S(1)} %copy-done.36, ...), custom_call_target="tpu_custom_call" | custom-call | flops 11500000256 | bytes 1048576 | tf_op jit(solution)/shard_map/attend_back_rest/pallas_call | solution.py:848
  164.4 4.6 %collective-permute-start.28 = (bf16[16,64,512]{2,1,0:T(8,128)(2,1)S(1)}, bf16[16,64,512]{2,1,0:T(8,128)(2,1)S(1)}, u32[]{:S(2)}, u32[]{:S(2)}) collective-permute-start(bf16[16,64,512]{2,1,0:T(8,128)(2,1)S(1)} %get-tuple-element.315), channel_id=1, source_target_pairs={{0,16},{16,0},{1,17},{17,1},{2,18},{18,2},{3,19},{19,3},{4,20},{20... | collective-permute-start | bytes 3145736 | tf_op jit(solution)/shard_map/ppermute | solution.py:994
  169.0 3.6 %input_grads.1 = (f32[512,512]{1,0:T(8,128)S(1)}, f32[8,512]{1,0:T(8,128)S(1)}) custom-call(s32[4]{0:T(128)S(1)} %copy-done.8, bf16[16384,512]{1,0:T(8,128)(2,1)} %get-tuple-element.290.refs_3_.refs_1_, bf16[512,256]{1,0:T(8,128)(2,1)S(1)} %get-tuple-element.302.refs_2_, bf16[768,256]{1,0:T(8,128)(2,1)S(1)} %get-tuple-element.303.refs_3_, ...), custom_call_target="tpu_custom_call" | custom-call | flops 5750000128 | bytes 1048576 | tf_op jit(solution)/shard_map/input_grads/pallas_call | solution.py:862
  174.0 1.5 collective-permute-start.29
  175.5 11.1 %feed_backward.1 = (bf16[16,144,512]{2,1,0:T(8,128)(2,1)}, bf16[16,144,512]{2,1,0:T(8,128)(2,1)}, f32[512,512]{1,0:T(8,128)S(1)}, bf16[512,512]{1,0:T(8,128)(2,1)S(1)}, f32[8,512]{1,0:T(8,128)S(1)}) custom-call(s32[4]{0:T(128)S(1)} %copy-done.8, f32[512,512]{1,0:T(8,128)S(1)} %get-tuple-element.316.grad_out, f32[16,512]{1,0:T(8,128)S(1)} %copy-done.6, ...), custom_call_target="tpu_custom_call" | custom-call | flops 14949999616 | bytes 1048576 | tf_op jit(solution)/shard_map/feed_backward/pallas_call | solution.py:906
  186.6 3.4 %collective-permute-done.29 = bf16[4,176,512]{2,1,0:T(8,128)(2,1)S(1)} collective-permute-done((bf16[4,176,512]{2,1,0:T(8,128)(2,1)S(1)}, bf16[4,176,512]{2,1,0:T(8,128)(2,1)S(1)}, u32[]{:S(2)}, u32[]{:S(2)}) %collective-permute-start.29) | collective-permute-done | bytes 720928 | tf_op jit(solution)/shard_map/ppermute | solution.py:990
  190.3 1.5 collective-permute-start.32
  191.8 1.2 add_convert_fusion.6
  193.8 6.7 %attend_back.3 = (bf16[512,256]{1,0:T(8,128)(2,1)S(1)}, bf16[768,256]{1,0:T(8,128)(2,1)S(1)}, bf16[768,256]{1,0:T(8,128)(2,1)S(1)}, bf16[4,512,256]{2,1,0:T(8,128)(2,1)S(1)}, f32[8,256]{1,0:T(8,128)S(1)}) custom-call(s32[4]{0:T(128)S(1)} %copy-done.8, bf16[512,512]{1,0:T(8,128)(2,1)S(1)} %get-tuple-element.326.refs_1_, ...), custom_call_target="tpu_custom_call" | custom-call | flops 10350000128 | bytes 1048576 | tf_op jit(solution)/shard_map/attend_back/pallas_call | solution.py:834
  200.5 2.9 %collective-permute-done.31 = bf16[2,176,512]{2,1,0:T(8,128)(2,1)S(1)} collective-permute-done((bf16[2,176,512]{2,1,0:T(8,128)(2,1)S(1)}, bf16[2,176,512]{2,1,0:T(8,128)(2,1)S(1)}, u32[]{:S(2)}, u32[]{:S(2)}) %collective-permute-start.31) | collective-permute-done | bytes 360480 | tf_op jit(solution)/shard_map/ppermute | solution.py:990
  203.5 1.7 collective-permute-start.35
  207.3 1.8 collective-permute-start.34
  209.1 9.6 %attend_back_rest.3 = (bf16[512,256]{1,0:T(8,128)(2,1)S(1)}, bf16[768,256]{1,0:T(8,128)(2,1)S(1)}, bf16[768,256]{1,0:T(8,128)(2,1)S(1)}, f32[8,256]{1,0:T(8,128)...) custom-call(s32[4]{0:T(128)S(1)} %copy-done.8, ...), custom_call_target="tpu_custom_call" | custom-call | flops 11500000256 | bytes 1048576 | tf_op jit(solution)/shard_map/attend_back_rest/pallas_call | solution.py:848
  218.7 3.1 %collective-permute-done.36 = bf16[8,144,512]{2,1,0:T(8,128)(2,1)S(1)} collective-permute-done((bf16[8,144,512]{2,1,0:T(8,128)(2,1)S(1)}, bf16[8,144,512]{2,1,0:T(8,128)(2,1)S(1)}, u32[]{:S(2)}, u32[]{:S(2)}) %collective-permute-start.36) | collective-permute-done | bytes 1179680 | tf_op jit(solution)/shard_map/ppermute | solution.py:990
  222.8 1.8 collective-permute-start.37
  225.6 5.1 %input_grads_last.1 = (bf16[16,16,512]{2,1,0:T(8,128)(2,1)S(1)}, bf16[16,16,512]{2,1,0:T(8,128)(2,1)S(1)}) custom-call(s32[4]{0:T(128)S(1)} %copy-done.8, bf16[16384,512]{1,0:T(8,128)(2,1)} %get-tuple-element.327.refs_3_.refs_1_, bf16[512,256]{1,0:T(8,128)(2,1)S(1)} %get-tuple-element.348.refs_2_, bf16[768,256]{1,0:T(8,128)(2,1)S(1)} %get-tuple-element.349.refs_3_, ...), custom_call_target="tpu_custom_call" | custom-call | flops 5750000128 | bytes 1048576 | tf_op jit(solution)/shard_map/input_grads_last/pallas_call | solution.py:875
  231.0 1.4 collective-permute-done.39
  233.4 1.3 collective-permute-done.41
  237.4 5.8 %collective-permute-done.42 = bf16[2,144,512]{2,1,0:T(8,128)(2,1)S(1)} collective-permute-done((bf16[2,144,512]{2,1,0:T(8,128)(2,1)S(1)}, bf16[2,144,512]{2,1,0:T(8,128)(2,1)S(1)}, u32[]{:S(2)}, u32[]{:S(2)}) %collective-permute-start.42) | collective-permute-done | bytes 294944 | tf_op jit(solution)/shard_map/ppermute | solution.py:990
  243.4 1.2 collective-permute-start.43
  244.9 1.3 collective-permute-start.45
  246.1 4.4 %collective-permute-done.43 = bf16[4,80,512]{2,1,0:T(8,128)(2,1)S(1)} collective-permute-done((bf16[4,80,512]{2,1,0:T(8,128)(2,1)S(1)}, bf16[4,80,512]{2,1,0:T(8,128)(2,1)S(1)}, u32[]{:S(2)}, u32[]{:S(2)}) %collective-permute-start.43) | collective-permute-done | bytes 327712 | tf_op jit(solution)/shard_map/ppermute | solution.py:990
  251.2 5.7 %collective-permute-done.44 = bf16[2,80,512]{2,1,0:T(8,128)(2,1)S(1)} collective-permute-done((bf16[2,80,512]{2,1,0:T(8,128)(2,1)S(1)}, bf16[2,80,512]{2,1,0:T(8,128)(2,1)S(1)}, u32[]{:S(2)}, u32[]{:S(2)}) %collective-permute-start.44) | collective-permute-done | bytes 163872 | tf_op jit(solution)/shard_map/ppermute | solution.py:990
  257.4 5.0 %collective-permute-done.46.refs_8_ = bf16[1,80,512]{2,1,0:T(8,128)(2,1)S(1)} collective-permute-done((bf16[1,80,512]{2,1,0:T(8,128)(2,1)S(1)}, bf16[1,80,512]{2,1,0:T(8,128)(2,1)S(1)}, u32[]{:S(2)}, u32[]{:S(2)}) %collective-permute-start.46) | collective-permute-done | bytes 81952 | tf_op jit(solution)/shard_map/ppermute | solution.py:990
  262.7 1.7 finish.1
  265.0 1.4 collective-permute-done.47
  266.4 1.7 collective-permute-start.50
  268.1 2.7 collective-permute-start.48
  272.6 1.9 collective-permute-start.53
  279.2 2.6 update.1
  (257 shorter events, 36.7 us)
Async XLA Ops:
  4.1 1.8 collective-permute-start
  6.9 8.5 %collective-permute-start.1 = (bf16[1,80,512]{2,1,0:T(8,128)(2,1)S(1)}, bf16[1,80,512]{2,1,0:T(8,128)(2,1)S(1)}, u32[]{:S(2)}, u32[]{:S(2)}) collective-permute-start(bf16[1,80,512]{2,1,0:T(8,128)(2,1)S(1)} %select_bitcast_fusion), channel_id=1, source_target_pairs={{0,8},{1,9},{2,10},{3,11},{4,12},{5,13},{6,14},{7,15},{8,0},{9,1},... | collective-permute-start | bytes 245768 | tf_op jit(solution)/shard_map/ppermute | solution.py:990
  15.4 5.8 %collective-permute-start.2 = (bf16[2,80,512]{2,1,0:T(8,128)(2,1)S(1)}, bf16[2,80,512]{2,1,0:T(8,128)(2,1)S(1)}, u32[]{:S(2)}, u32[]{:S(2)}) collective-permute-start(bf16[2,80,512]{2,1,0:T(8,128)(2,1)S(1)} %constant_dynamic-update-slice_fusion), channel_id=1, source_target_pairs={{0,4},{1,5},{2,6},{3,7},{4,0},{5,1},{6,2},{7,3},{8,12},{9,13},{10,... | collective-permute-start | bytes 491528 | tf_op jit(solution)/shard_map/ppermute | solution.py:990
  21.2 9.4 %collective-permute-start.4 = (bf16[1,144,512]{2,1,0:T(8,128)(2,1)S(1)}, bf16[1,144,512]{2,1,0:T(8,128)(2,1)S(1)}, u32[]{:S(2)}, u32[]{:S(2)}) collective-permute-start(bf16[1,144,512]{2,1,0:T(8,128)(2,1)S(1)} %fusion.2), channel_id=1, source_target_pairs={{0,8},{1,9},{2,10},{3,11},{4,12},{5,13},{6,14},{7,15},{8,0},{9,1},... | collective-permute-start | bytes 442376 | tf_op jit(solution)/shard_map/ppermute | solution.py:990
  24.0 7.1 %collective-permute-start.3 = (bf16[4,80,512]{2,1,0:T(8,128)(2,1)S(1)}, bf16[4,80,512]{2,1,0:T(8,128)(2,1)S(1)}, u32[]{:S(2)}, u32[]{:S(2)}) collective-permute-start(bf16[4,80,512]{2,1,0:T(8,128)(2,1)S(1)} %constant_dynamic-update-slice_fusion.2), channel_id=1, source_target_pairs={{0,1},{1,0},{2,3},{3,2},{4,5},{5,4},{6,7},{7,6},{8,9},{9,8},{10,11... | collective-permute-start | bytes 983048 | tf_op jit(solution)/shard_map/ppermute | solution.py:990
  31.2 10.7 %collective-permute-start.5 = (bf16[8,80,512]{2,1,0:T(8,128)(2,1)S(1)}, bf16[8,80,512]{2,1,0:T(8,128)(2,1)S(1)}, u32[]{:S(2)}, u32[]{:S(2)}) collective-permute-start(bf16[8,80,512]{2,1,0:T(8,128)(2,1)S(1)} %constant_dynamic-update-slice_fusion.4.refs_2_), channel_id=1, source_target_pairs={{0,2},{1,3},{2,0},{3,1},{4,6},{5,7},{6,4},{7,5},{8,10},{9,11},{10,... | collective-permute-start | bytes 1966088 | tf_op jit(solution)/shard_map/ppermute | solution.py:990
  32.8 8.7 %collective-permute-start.6 = (bf16[2,144,512]{2,1,0:T(8,128)(2,1)S(1)}, bf16[2,144,512]{2,1,0:T(8,128)(2,1)S(1)}, u32[]{:S(2)}, u32[]{:S(2)}) collective-permute-start(bf16[2,144,512]{2,1,0:T(8,128)(2,1)S(1)} %constant_dynamic-update-slice_fusion.6), channel_id=1, source_target_pairs={{0,4},{1,5},{2,6},{3,7},{4,0},{5,1},{6,2},{7,3},{8,12},{9,13},{10,... | collective-permute-start | bytes 884744 | tf_op jit(solution)/shard_map/ppermute | solution.py:990
  34.6 5.9 %collective-permute-start.7 = (bf16[1,64,512]{2,1,0:T(8,128)(2,1)S(1)}, bf16[1,64,512]{2,1,0:T(8,128)(2,1)S(1)}, u32[]{:S(2)}, u32[]{:S(2)}) collective-permute-start(bf16[1,64,512]{2,1,0:T(8,128)(2,1)S(1)} %slice_bitcast_fusion), channel_id=1, source_target_pairs={{0,8},{1,9},{2,10},{3,11},{4,12},{5,13},{6,14},{7,15},{8,0},{9,1},... | collective-permute-start | bytes 196616 | tf_op jit(solution)/shard_map/ppermute | solution.py:990
  41.9 10.6 %collective-permute-start.8 = (bf16[8,80,512]{2,1,0:T(8,128)(2,1)S(1)}, bf16[8,80,512]{2,1,0:T(8,128)(2,1)S(1)}, u32[]{:S(2)}, u32[]{:S(2)}) collective-permute-start(bf16[8,80,512]{2,1,0:T(8,128)(2,1)S(1)} %constant_dynamic-update-slice_fusion.4.refs_2_), channel_id=1, source_target_pairs={{0,16},{16,0},{1,17},{17,1},{2,18},{18,2},{3,19},{19,3},{4,20},{20... | collective-permute-start | bytes 1966088 | tf_op jit(solution)/shard_map/ppermute | solution.py:994
  42.0 10.5 %collective-permute-start.9 = (bf16[8,80,512]{2,1,0:T(8,128)(2,1)S(1)}, bf16[8,80,512]{2,1,0:T(8,128)(2,1)S(1)}, u32[]{:S(2)}, u32[]{:S(2)}) collective-permute-start(bf16[8,80,512]{2,1,0:T(8,128)(2,1)S(1)} %collective-permute-done.5.refs_3_), channel_id=1, source_target_pairs={{0,16},{16,0},{1,17},{17,1},{2,18},{18,2},{3,19},{19,3},{4,20},{20... | collective-permute-start | bytes 1966088 | tf_op jit(solution)/shard_map/ppermute | solution.py:994
  42.5 9.9 %collective-permute-start.10 = (bf16[4,144,512]{2,1,0:T(8,128)(2,1)S(1)}, bf16[4,144,512]{2,1,0:T(8,128)(2,1)S(1)}, u32[]{:S(2)}, u32[]{:S(2)}) collective-permute-start(bf16[4,144,512]{2,1,0:T(8,128)(2,1)S(1)} %constant_dynamic-update-slice_fusion.8), channel_id=1, source_target_pairs={{0,1},{1,0},{2,3},{3,2},{4,5},{5,4},{6,7},{7,6},{8,9},{9,8},{10,11... | collective-permute-start | bytes 1769480 | tf_op jit(solution)/shard_map/ppermute | solution.py:990
  44.1 6.4 %collective-permute-start.11 = (bf16[2,64,512]{2,1,0:T(8,128)(2,1)S(1)}, bf16[2,64,512]{2,1,0:T(8,128)(2,1)S(1)}, u32[]{:S(2)}, u32[]{:S(2)}) collective-permute-start(bf16[2,64,512]{2,1,0:T(8,128)(2,1)S(1)} %constant_dynamic-update-slice_fusion.10), channel_id=1, source_target_pairs={{0,4},{1,5},{2,6},{3,7},{4,0},{5,1},{6,2},{7,3},{8,12},{9,13},{10,... | collective-permute-start | bytes 393224 | tf_op jit(solution)/shard_map/ppermute | solution.py:990
  52.5 13.1 %collective-permute-start.14 = (bf16[8,144,512]{2,1,0:T(8,128)(2,1)S(1)}, bf16[8,144,512]{2,1,0:T(8,128)(2,1)S(1)}, u32[]{:S(2)}, u32[]{:S(2)}) collective-permute-start(bf16[8,144,512]{2,1,0:T(8,128)(2,1)S(1)} %constant_dynamic-update-slice_fusion.12.own_low), channel_id=1, source_target_pairs={{0,16},{16,0},{1,17},{17,1},{2,18},{18,2},{3,19},{19,3},{4,20},{20... | collective-permute-start | bytes 3538952 | tf_op jit(solution)/shard_map/ppermute | solution.py:994
  52.6 22.5 %collective-permute-start.15 = (bf16[8,144,512]{2,1,0:T(8,128)(2,1)S(1)}, bf16[8,144,512]{2,1,0:T(8,128)(2,1)S(1)}, u32[]{:S(2)}, u32[]{:S(2)}) collective-permute-start(bf16[8,144,512]{2,1,0:T(8,128)(2,1)S(1)} %constant_dynamic-update-slice_fusion.12.own_low), channel_id=1, source_target_pairs={{0,2},{1,3},{2,0},{3,1},{4,6},{5,7},{6,4},{7,5},{8,10},{9,11},{10,... | collective-permute-start | bytes 3538952 | tf_op jit(solution)/shard_map/ppermute | solution.py:990
  54.2 11.3 %collective-permute-start.13 = (bf16[1,176,512]{2,1,0:T(8,128)(2,1)S(1)}, bf16[1,176,512]{2,1,0:T(8,128)(2,1)S(1)}, u32[]{:S(2)}, u32[]{:S(2)}) collective-permute-start(bf16[1,176,512]{2,1,0:T(8,128)(2,1)S(1)} %maximum_bitcast_fusion), channel_id=1, source_target_pairs={{0,8},{1,9},{2,10},{3,11},{4,12},{5,13},{6,14},{7,15},{8,0},{9,1},... | collective-permute-start | bytes 540680 | tf_op jit(solution)/shard_map/ppermute | solution.py:990
  56.3 9.3 %collective-permute-start.12 = (bf16[4,64,512]{2,1,0:T(8,128)(2,1)S(1)}, bf16[4,64,512]{2,1,0:T(8,128)(2,1)S(1)}, u32[]{:S(2)}, u32[]{:S(2)}) collective-permute-start(bf16[4,64,512]{2,1,0:T(8,128)(2,1)S(1)} %pad_maximum_fusion.5), channel_id=1, source_target_pairs={{0,1},{1,0},{2,3},{3,2},{4,5},{5,4},{6,7},{7,6},{8,9},{9,8},{10,11... | collective-permute-start | bytes 786440 | tf_op jit(solution)/shard_map/ppermute | solution.py:990
  63.7 31.6 %copy-start.5 = (f32[16,512]{1,0:T(8,128)}, f32[16,512]{1,0:T(8,128)S(1)}, u32[]{:S(2)}) copy-start(f32[16,512]{1,0:T(8,128)S(1)} %get-tuple-element.264.vecs.refs_3_.refs_11_) | copy-start | bytes 98308
  65.7 12.0 %collective-permute-start.18 = (bf16[8,64,512]{2,1,0:T(8,128)(2,1)S(1)}, bf16[8,64,512]{2,1,0:T(8,128)(2,1)S(1)}, u32[]{:S(2)}, u32[]{:S(2)}) collective-permute-start(bf16[8,64,512]{2,1,0:T(8,128)(2,1)S(1)} %constant_dynamic-update-slice_fusion.14.refs_4_), channel_id=1, source_target_pairs={{0,16},{16,0},{1,17},{17,1},{2,18},{18,2},{3,19},{19,3},{4,20},{20... | collective-permute-start | bytes 1572872 | tf_op jit(solution)/shard_map/ppermute | solution.py:994
  65.8 11.9 %collective-permute-start.16 = (bf16[8,64,512]{2,1,0:T(8,128)(2,1)S(1)}, bf16[8,64,512]{2,1,0:T(8,128)(2,1)S(1)}, u32[]{:S(2)}, u32[]{:S(2)}) collective-permute-start(bf16[8,64,512]{2,1,0:T(8,128)(2,1)S(1)} %constant_dynamic-update-slice_fusion.14.refs_4_), channel_id=1, source_target_pairs={{0,2},{1,3},{2,0},{3,1},{4,6},{5,7},{6,4},{7,5},{8,10},{9,11},{10,... | collective-permute-start | bytes 1572872 | tf_op jit(solution)/shard_map/ppermute | solution.py:990
  67.0 10.7 %collective-permute-start.17 = (bf16[2,176,512]{2,1,0:T(8,128)(2,1)S(1)}, bf16[2,176,512]{2,1,0:T(8,128)(2,1)S(1)}, u32[]{:S(2)}, u32[]{:S(2)}) collective-permute-start(bf16[2,176,512]{2,1,0:T(8,128)(2,1)S(1)} %pad_maximum_fusion.3), channel_id=1, source_target_pairs={{0,4},{1,5},{2,6},{3,7},{4,0},{5,1},{6,2},{7,3},{8,12},{9,13},{10,... | collective-permute-start | bytes 1081352 | tf_op jit(solution)/shard_map/ppermute | solution.py:990
  77.7 3.5 %collective-permute-start.19 = (bf16[8,144,512]{2,1,0:T(8,128)(2,1)S(1)}, bf16[8,144,512]{2,1,0:T(8,128)(2,1)S(1)}, u32[]{:S(2)}, u32[]{:S(2)}) collective-permute-start(bf16[8,144,512]{2,1,0:T(8,128)(2,1)S(1)} %collective-permute-done.15.own_high), channel_id=1, source_target_pairs={{0,16},{16,0},{1,17},{17,1},{2,18},{18,2},{3,19},{19,3},{4,20},{20... | collective-permute-start | bytes 3538952 | tf_op jit(solution)/shard_map/ppermute | solution.py:994
  78.7 12.8 %collective-permute-start.21 = (bf16[8,64,512]{2,1,0:T(8,128)(2,1)S(1)}, bf16[8,64,512]{2,1,0:T(8,128)(2,1)S(1)}, u32[]{:S(2)}, u32[]{:S(2)}) collective-permute-start(bf16[8,64,512]{2,1,0:T(8,128)(2,1)S(1)} %collective-permute-done.16.refs_5_), channel_id=1, source_target_pairs={{0,16},{16,0},{1,17},{17,1},{2,18},{18,2},{3,19},{19,3},{4,20},{20... | collective-permute-start | bytes 1572872 | tf_op jit(solution)/shard_map/ppermute | solution.py:994
  78.8 12.7 %collective-permute-start.20 = (bf16[4,176,512]{2,1,0:T(8,128)(2,1)S(1)}, bf16[4,176,512]{2,1,0:T(8,128)(2,1)S(1)}, u32[]{:S(2)}, u32[]{:S(2)}) collective-permute-start(bf16[4,176,512]{2,1,0:T(8,128)(2,1)S(1)} %pad_maximum_fusion.1), channel_id=1, source_target_pairs={{0,1},{1,0},{2,3},{3,2},{4,5},{5,4},{6,7},{7,6},{8,9},{9,8},{10,11... | collective-permute-start | bytes 2162696 | tf_op jit(solution)/shard_map/ppermute | solution.py:990
  91.5 3.8 %collective-permute-start.22 = (f32[256,512]{1,0:T(8,128)S(1)}, f32[256,512]{1,0:T(8,128)S(1)}, u32[]{:S(2)}, u32[]{:S(2)}) collective-permute-start(f32[256,512]{1,0:T(8,128)S(1)} %get-tuple-element.273), channel_id=1, source_target_pairs={{0,16},{1,17},{2,18},{3,19},{4,20},{5,21},{6,22},{7,23},{8,24},{9,... | collective-permute-start | bytes 1572872 | tf_op jit(solution)/shard_map/ppermute | solution.py:1192
  94.0 22.6 %collective-permute-start.24 = (bf16[8,176,512]{2,1,0:T(8,128)(2,1)S(1)}, bf16[8,176,512]{2,1,0:T(8,128)(2,1)S(1)}, u32[]{:S(2)}, u32[]{:S(2)}) collective-permute-start(bf16[8,176,512]{2,1,0:T(8,128)(2,1)S(1)} %constant_dynamic-update-slice_fusion.17.own_low), channel_id=1, source_target_pairs={{0,16},{16,0},{1,17},{17,1},{2,18},{18,2},{3,19},{19,3},{4,20},{20... | collective-permute-start | bytes 4325384 | tf_op jit(solution)/shard_map/ppermute | solution.py:994
  94.1 22.6 %collective-permute-start.23 = (bf16[8,176,512]{2,1,0:T(8,128)(2,1)S(1)}, bf16[8,176,512]{2,1,0:T(8,128)(2,1)S(1)}, u32[]{:S(2)}, u32[]{:S(2)}) collective-permute-start(bf16[8,176,512]{2,1,0:T(8,128)(2,1)S(1)} %constant_dynamic-update-slice_fusion.17.own_low), channel_id=1, source_target_pairs={{0,2},{1,3},{2,0},{3,1},{4,6},{5,7},{6,4},{7,5},{8,10},{9,11},{10,... | collective-permute-start | bytes 4325384 | tf_op jit(solution)/shard_map/ppermute | solution.py:990
  118.9 26.7 %copy-start.8 = (s32[4]{0:T(128)S(1)}, s32[4]{0:T(128)}, u32[]{:S(2)}) copy-start(s32[4]{0:T(128)} %pad_add_fusion.scalars.refs_0_) | copy-start | bytes 52
  118.9 6.9 %collective-permute-start.25 = (bf16[8,176,512]{2,1,0:T(8,128)(2,1)S(1)}, bf16[8,176,512]{2,1,0:T(8,128)(2,1)S(1)}, u32[]{:S(2)}, u32[]{:S(2)}) collective-permute-start(bf16[8,176,512]{2,1,0:T(8,128)(2,1)S(1)} %collective-permute-done.23.own_high), channel_id=1, source_target_pairs={{0,16},{16,0},{1,17},{17,1},{2,18},{18,2},{3,19},{19,3},{4,20},{20... | collective-permute-start | bytes 4325384 | tf_op jit(solution)/shard_map/ppermute | solution.py:994
  145.2 8.3 %collective-permute-start.26 = (bf16[16,176,512]{2,1,0:T(8,128)(2,1)}, bf16[16,176,512]{2,1,0:T(8,128)(2,1)S(1)}, u32[]{:S(2)}, u32[]{:S(2)}) collective-permute-start(bf16[16,176,512]{2,1,0:T(8,128)(2,1)} %get-tuple-element.301), channel_id=1, source_target_pairs={{0,16},{16,0},{1,17},{17,1},{2,18},{18,2},{3,19},{19,3},{4,20},{20... | collective-permute-start | bytes 8650760 | tf_op jit(solution)/shard_map/ppermute | solution.py:994
  153.5 20.3 %copy-start.43 = (bf16[16,176,512]{2,1,0:T(8,128)(2,1)}, bf16[16,176,512]{2,1,0:T(8,128)(2,1)S(1)}, u32[]{:S(2)}) copy-start(bf16[16,176,512]{2,1,0:T(8,128)(2,1)S(1)} %collective-permute-done.26) | copy-start | bytes 8650756
  153.9 19.1 %collective-permute-start.27 = (bf16[8,176,512]{2,1,0:T(8,128)(2,1)S(1)}, bf16[8,176,512]{2,1,0:T(8,128)(2,1)S(1)}, u32[]{:S(2)}, u32[]{:S(2)}) collective-permute-start(bf16[8,176,512]{2,1,0:T(8,128)(2,1)S(1)} %add_convert_fusion), channel_id=1, source_target_pairs={{0,2},{1,3},{2,0},{3,1},{4,6},{5,7},{6,4},{7,5},{8,10},{9,11},{10,... | collective-permute-start | bytes 4325384 | tf_op jit(solution)/shard_map/ppermute | solution.py:990
  164.4 8.2 %collective-permute-start.28 = (bf16[16,64,512]{2,1,0:T(8,128)(2,1)S(1)}, bf16[16,64,512]{2,1,0:T(8,128)(2,1)S(1)}, u32[]{:S(2)}, u32[]{:S(2)}) collective-permute-start(bf16[16,64,512]{2,1,0:T(8,128)(2,1)S(1)} %get-tuple-element.315), channel_id=1, source_target_pairs={{0,16},{16,0},{1,17},{17,1},{2,18},{18,2},{3,19},{19,3},{4,20},{20... | collective-permute-start | bytes 3145736 | tf_op jit(solution)/shard_map/ppermute | solution.py:994
  173.2 13.5 %collective-permute-start.30 = (bf16[8,64,512]{2,1,0:T(8,128)(2,1)S(1)}, bf16[8,64,512]{2,1,0:T(8,128)(2,1)S(1)}, u32[]{:S(2)}, u32[]{:S(2)}) collective-permute-start(bf16[8,64,512]{2,1,0:T(8,128)(2,1)S(1)} %add_convert_fusion.5), channel_id=1, source_target_pairs={{0,2},{1,3},{2,0},{3,1},{4,6},{5,7},{6,4},{7,5},{8,10},{9,11},{10,... | collective-permute-start | bytes 1572872 | tf_op jit(solution)/shard_map/ppermute | solution.py:990
  174.0 16.0 %collective-permute-start.29 = (bf16[4,176,512]{2,1,0:T(8,128)(2,1)S(1)}, bf16[4,176,512]{2,1,0:T(8,128)(2,1)S(1)}, u32[]{:S(2)}, u32[]{:S(2)}) collective-permute-start(bf16[4,176,512]{2,1,0:T(8,128)(2,1)S(1)} %add_convert_fusion.2), channel_id=1, source_target_pairs={{0,1},{1,0},{2,3},{3,2},{4,5},{5,4},{6,7},{7,6},{8,9},{9,8},{10,11... | collective-permute-start | bytes 2162696 | tf_op jit(solution)/shard_map/ppermute | solution.py:990
  186.6 16.8 %copy-start.47 = (bf16[8,64,512]{2,1,0:T(8,128)(2,1)}, bf16[8,64,512]{2,1,0:T(8,128)(2,1)S(1)}, u32[]{:S(2)}) copy-start(bf16[8,64,512]{2,1,0:T(8,128)(2,1)S(1)} %collective-permute-done.30) | copy-start | bytes 1572868
  190.1 13.3 %collective-permute-start.33 = (bf16[16,144,512]{2,1,0:T(8,128)(2,1)}, bf16[16,144,512]{2,1,0:T(8,128)(2,1)S(1)}, u32[]{:S(2)}, u32[]{:S(2)}) collective-permute-start(bf16[16,144,512]{2,1,0:T(8,128)(2,1)} %get-tuple-element.335), channel_id=1, source_target_pairs={{0,16},{16,0},{1,17},{17,1},{2,18},{18,2},{3,19},{19,3},{4,20},{20... | collective-permute-start | bytes 7077896 | tf_op jit(solution)/shard_map/ppermute | solution.py:994
  190.3 10.2 %collective-permute-start.32 = (bf16[4,64,512]{2,1,0:T(8,128)(2,1)S(1)}, bf16[4,64,512]{2,1,0:T(8,128)(2,1)S(1)}, u32[]{:S(2)}, u32[]{:S(2)}) collective-permute-start(bf16[4,64,512]{2,1,0:T(8,128)(2,1)S(1)} %add_convert_fusion.9), channel_id=1, source_target_pairs={{0,1},{1,0},{2,3},{3,2},{4,5},{5,4},{6,7},{7,6},{8,9},{9,8},{10,11... | collective-permute-start | bytes 786440 | tf_op jit(solution)/shard_map/ppermute | solution.py:990
  193.0 10.4 %collective-permute-start.31 = (bf16[2,176,512]{2,1,0:T(8,128)(2,1)S(1)}, bf16[2,176,512]{2,1,0:T(8,128)(2,1)S(1)}, u32[]{:S(2)}, u32[]{:S(2)}) collective-permute-start(bf16[2,176,512]{2,1,0:T(8,128)(2,1)S(1)} %add_convert_fusion.6), channel_id=1, source_target_pairs={{0,4},{1,5},{2,6},{3,7},{4,0},{5,1},{6,2},{7,3},{8,12},{9,13},{10,... | collective-permute-start | bytes 1081352 | tf_op jit(solution)/shard_map/ppermute | solution.py:990
  203.5 15.2 %collective-permute-start.35 = (bf16[2,64,512]{2,1,0:T(8,128)(2,1)S(1)}, bf16[2,64,512]{2,1,0:T(8,128)(2,1)S(1)}, u32[]{:S(2)}, u32[]{:S(2)}) collective-permute-start(bf16[2,64,512]{2,1,0:T(8,128)(2,1)S(1)} %add_convert_fusion.14), channel_id=1, source_target_pairs={{0,4},{1,5},{2,6},{3,7},{4,0},{5,1},{6,2},{7,3},{8,12},{9,13},{10,... | collective-permute-start | bytes 393224 | tf_op jit(solution)/shard_map/ppermute | solution.py:990
  205.6 16.3 %collective-permute-start.36 = (bf16[8,144,512]{2,1,0:T(8,128)(2,1)S(1)}, bf16[8,144,512]{2,1,0:T(8,128)(2,1)S(1)}, u32[]{:S(2)}, u32[]{:S(2)}) collective-permute-start(bf16[8,144,512]{2,1,0:T(8,128)(2,1)S(1)} %add_convert_fusion.1), channel_id=1, source_target_pairs={{0,2},{1,3},{2,0},{3,1},{4,6},{5,7},{6,4},{7,5},{8,10},{9,11},{10,... | collective-permute-start | bytes 3538952 | tf_op jit(solution)/shard_map/ppermute | solution.py:990
  207.3 11.4 %collective-permute-start.34 = (bf16[1,176,512]{2,1,0:T(8,128)(2,1)S(1)}, bf16[1,176,512]{2,1,0:T(8,128)(2,1)S(1)}, u32[]{:S(2)}, u32[]{:S(2)}) collective-permute-start(bf16[1,176,512]{2,1,0:T(8,128)(2,1)S(1)} %add_convert_fusion.10), channel_id=1, source_target_pairs={{0,8},{1,9},{2,10},{3,11},{4,12},{5,13},{6,14},{7,15},{8,0},{9,1},... | collective-permute-start | bytes 540680 | tf_op jit(solution)/shard_map/ppermute | solution.py:990
  221.9 8.9 %collective-permute-start.38 = (bf16[16,64,512]{2,1,0:T(8,128)(2,1)S(1)}, bf16[16,64,512]{2,1,0:T(8,128)(2,1)S(1)}, u32[]{:S(2)}, u32[]{:S(2)}) collective-permute-start(bf16[16,64,512]{2,1,0:T(8,128)(2,1)S(1)} %get-tuple-element.364), channel_id=1, source_target_pairs={{0,16},{16,0},{1,17},{17,1},{2,18},{18,2},{3,19},{19,3},{4,20},{20... | collective-permute-start | bytes 3145736 | tf_op jit(solution)/shard_map/ppermute | solution.py:994
  222.8 8.0 %collective-permute-start.37 = (bf16[1,64,512]{2,1,0:T(8,128)(2,1)S(1)}, bf16[1,64,512]{2,1,0:T(8,128)(2,1)S(1)}, u32[]{:S(2)}, u32[]{:S(2)}) collective-permute-start(bf16[1,64,512]{2,1,0:T(8,128)(2,1)S(1)} %add_convert_fusion.17), channel_id=1, source_target_pairs={{0,8},{1,9},{2,10},{3,11},{4,12},{5,13},{6,14},{7,15},{8,0},{9,1},... | collective-permute-start | bytes 196616 | tf_op jit(solution)/shard_map/ppermute | solution.py:990
  224.8 9.9 %collective-permute-start.41 = (bf16[4,144,512]{2,1,0:T(8,128)(2,1)S(1)}, bf16[4,144,512]{2,1,0:T(8,128)(2,1)S(1)}, u32[]{:S(2)}, u32[]{:S(2)}) collective-permute-start(bf16[4,144,512]{2,1,0:T(8,128)(2,1)S(1)} %add_convert_fusion.3), channel_id=1, source_target_pairs={{0,1},{1,0},{2,3},{3,2},{4,5},{5,4},{6,7},{7,6},{8,9},{9,8},{10,11... | collective-permute-start | bytes 1769480 | tf_op jit(solution)/shard_map/ppermute | solution.py:990
  230.7 1.6 collective-permute-start.39
  232.5 10.8 %collective-permute-start.40 = (bf16[8,80,512]{2,1,0:T(8,128)(2,1)S(1)}, bf16[8,80,512]{2,1,0:T(8,128)(2,1)S(1)}, u32[]{:S(2)}, u32[]{:S(2)}) collective-permute-start(bf16[8,80,512]{2,1,0:T(8,128)(2,1)S(1)} %pad_maximum_fusion.2), channel_id=1, source_target_pairs={{0,2},{1,3},{2,0},{3,1},{4,6},{5,7},{6,4},{7,5},{8,10},{9,11},{10,... | collective-permute-start | bytes 1966088 | tf_op jit(solution)/shard_map/ppermute | solution.py:990
  234.9 8.3 %collective-permute-start.42 = (bf16[2,144,512]{2,1,0:T(8,128)(2,1)S(1)}, bf16[2,144,512]{2,1,0:T(8,128)(2,1)S(1)}, u32[]{:S(2)}, u32[]{:S(2)}) collective-permute-start(bf16[2,144,512]{2,1,0:T(8,128)(2,1)S(1)} %add_convert_fusion.7), channel_id=1, source_target_pairs={{0,4},{1,5},{2,6},{3,7},{4,0},{5,1},{6,2},{7,3},{8,12},{9,13},{10,... | collective-permute-start | bytes 884744 | tf_op jit(solution)/shard_map/ppermute | solution.py:990
  243.4 7.1 %collective-permute-start.43 = (bf16[4,80,512]{2,1,0:T(8,128)(2,1)S(1)}, bf16[4,80,512]{2,1,0:T(8,128)(2,1)S(1)}, u32[]{:S(2)}, u32[]{:S(2)}) collective-permute-start(bf16[4,80,512]{2,1,0:T(8,128)(2,1)S(1)} %pad_maximum_fusion.4), channel_id=1, source_target_pairs={{0,1},{1,0},{2,3},{3,2},{4,5},{5,4},{6,7},{7,6},{8,9},{9,8},{10,11... | collective-permute-start | bytes 983048 | tf_op jit(solution)/shard_map/ppermute | solution.py:990
  244.9 17.5 %copy-start.41 = (f32[8,128]{1,0:T(8,128)S(1)}, f32[8,128]{1,0:T(8,128)}, u32[]{:S(2)}) copy-start(f32[8,128]{1,0:T(8,128)} %get-tuple-element.289.refs_1_) | copy-start | bytes 12292
  244.9 12.6 %collective-permute-start.45 = (bf16[1,144,512]{2,1,0:T(8,128)(2,1)S(1)}, bf16[1,144,512]{2,1,0:T(8,128)(2,1)S(1)}, u32[]{:S(2)}, u32[]{:S(2)}) collective-permute-start(bf16[1,144,512]{2,1,0:T(8,128)(2,1)S(1)} %get-tuple-element.411), channel_id=1, source_target_pairs={{0,8},{1,9},{2,10},{3,11},{4,12},{5,13},{6,14},{7,15},{8,0},{9,1},... | collective-permute-start | bytes 442376 | tf_op jit(solution)/shard_map/ppermute | solution.py:990
  250.7 6.2 %collective-permute-start.44 = (bf16[2,80,512]{2,1,0:T(8,128)(2,1)S(1)}, bf16[2,80,512]{2,1,0:T(8,128)(2,1)S(1)}, u32[]{:S(2)}, u32[]{:S(2)}) collective-permute-start(bf16[2,80,512]{2,1,0:T(8,128)(2,1)S(1)} %pad_maximum_fusion.6), channel_id=1, source_target_pairs={{0,4},{1,5},{2,6},{3,7},{4,0},{5,1},{6,2},{7,3},{8,12},{9,13},{10,... | collective-permute-start | bytes 491528 | tf_op jit(solution)/shard_map/ppermute | solution.py:990
  257.0 5.4 %collective-permute-start.46 = (bf16[1,80,512]{2,1,0:T(8,128)(2,1)S(1)}, bf16[1,80,512]{2,1,0:T(8,128)(2,1)S(1)}, u32[]{:S(2)}, u32[]{:S(2)}) collective-permute-start(bf16[1,80,512]{2,1,0:T(8,128)(2,1)S(1)} %pad_maximum_fusion.7), channel_id=1, source_target_pairs={{0,8},{1,9},{2,10},{3,11},{4,12},{5,13},{6,14},{7,15},{8,0},{9,1},... | collective-permute-start | bytes 245768 | tf_op jit(solution)/shard_map/ppermute | solution.py:990
  262.4 16.5 %copy-start.11 = (f32[1,32,2048]{2,1,0:T(8,128)S(1)}, f32[1,32,2048]{2,1,0:T(8,128)}, u32[]{:S(2)}) copy-start(f32[1,32,2048]{2,1,0:T(8,128)} %refs_12_.1) | copy-start | bytes 786436
  262.4 16.5 %copy-start.12 = (f32[1,128,512]{2,1,0:T(8,128)S(1)}, f32[1,128,512]{2,1,0:T(8,128)}, u32[]{:S(2)}) copy-start(f32[1,128,512]{2,1,0:T(8,128)} %refs_13_.1) | copy-start | bytes 786436
  262.4 16.5 %copy-start.13 = (f32[1,32,2048]{2,1,0:T(8,128)S(1)}, f32[1,32,2048]{2,1,0:T(8,128)}, u32[]{:S(2)}) copy-start(f32[1,32,2048]{2,1,0:T(8,128)} %refs_21_.1) | copy-start | bytes 786436
  262.4 16.5 %copy-start.14 = (f32[1,128,512]{2,1,0:T(8,128)S(1)}, f32[1,128,512]{2,1,0:T(8,128)}, u32[]{:S(2)}) copy-start(f32[1,128,512]{2,1,0:T(8,128)} %refs_22_.1) | copy-start | bytes 786436
  264.4 14.5 %collective-permute-start.54 = (f32[256,512]{1,0:T(8,128)S(1)}, f32[256,512]{1,0:T(8,128)S(1)}, u32[]{:S(2)}, u32[]{:S(2)}) collective-permute-start(f32[256,512]{1,0:T(8,128)S(1)} %get-tuple-element.381), channel_id=1, source_target_pairs={{0,16},{16,0},{1,17},{17,1},{2,18},{18,2},{3,19},{19,3},{4,20},{20... | collective-permute-start | bytes 1572872 | tf_op jit(solution)/shard_map/ppermute | solution.py:994
  264.5 1.9 collective-permute-start.47
  266.4 5.4 %collective-permute-start.50 = (f32[8,128]{1,0:T(8,128)S(1)}, f32[8,128]{1,0:T(8,128)S(1)}, u32[]{:S(2)}, u32[]{:S(2)}) collective-permute-start(f32[8,128]{1,0:T(8,128)S(1)} %add.323), channel_id=1, source_target_pairs={{0,12},{1,13},{2,14},{3,15},{4,8},{5,9},{6,10},{7,11},{8,4},{9,5},... | collective-permute-start | bytes 12296 | tf_op jit(solution)/shard_map/ppermute | solution.py:990
  268.1 3.7 %collective-permute-start.49 = (f32[8,128]{1,0:T(8,128)S(1)}, f32[8,128]{1,0:T(8,128)S(1)}, u32[]{:S(2)}, u32[]{:S(2)}) collective-permute-start(f32[8,128]{1,0:T(8,128)S(1)} %add.323), channel_id=1, source_target_pairs={{0,4},{1,5},{2,6},{3,7},{4,0},{5,1},{6,2},{7,3},{8,12},{9,13},{10,... | collective-permute-start | bytes 12296 | tf_op jit(solution)/shard_map/ppermute | solution.py:990
  268.1 4.5 %collective-permute-start.48 = (f32[8,128]{1,0:T(8,128)S(1)}, f32[8,128]{1,0:T(8,128)S(1)}, u32[]{:S(2)}, u32[]{:S(2)}) collective-permute-start(f32[8,128]{1,0:T(8,128)S(1)} %add.323), channel_id=1, source_target_pairs={{0,8},{1,9},{2,10},{3,11},{4,12},{5,13},{6,14},{7,15},{8,0},{9,1},... | collective-permute-start | bytes 12296 | tf_op jit(solution)/shard_map/ppermute | solution.py:990
  272.6 4.5 %collective-permute-start.53 = (f32[8,128]{1,0:T(8,128)S(1)}, f32[8,128]{1,0:T(8,128)S(1)}, u32[]{:S(2)}, u32[]{:S(2)}) collective-permute-start(f32[8,128]{1,0:T(8,128)S(1)} %add_add_fusion.1), channel_id=1, source_target_pairs={{0,3},{1,2},{2,1},{3,0},{4,7},{5,6},{6,5},{7,4},{8,11},{9,10},{10,... | collective-permute-start | bytes 12296 | tf_op jit(solution)/shard_map/ppermute | solution.py:990
  274.5 3.6 %collective-permute-start.52 = (f32[8,128]{1,0:T(8,128)S(1)}, f32[8,128]{1,0:T(8,128)S(1)}, u32[]{:S(2)}, u32[]{:S(2)}) collective-permute-start(f32[8,128]{1,0:T(8,128)S(1)} %add_add_fusion.1), channel_id=1, source_target_pairs={{0,2},{1,3},{2,0},{3,1},{4,6},{5,7},{6,4},{7,5},{8,10},{9,11},{10,... | collective-permute-start | bytes 12296 | tf_op jit(solution)/shard_map/ppermute | solution.py:990
  275.3 3.6 %collective-permute-start.51 = (f32[8,128]{1,0:T(8,128)S(1)}, f32[8,128]{1,0:T(8,128)S(1)}, u32[]{:S(2)}, u32[]{:S(2)}) collective-permute-start(f32[8,128]{1,0:T(8,128)S(1)} %add_add_fusion.1), channel_id=1, source_target_pairs={{0,1},{1,0},{2,3},{3,2},{4,5},{5,4},{6,7},{7,6},{8,9},{9,8},{10,11... | collective-permute-start | bytes 12296 | tf_op jit(solution)/shard_map/ppermute | solution.py:990
  (53 other events, 592.6 us)
